TPU v7x, 256 devices: a whole 4x4x8 slice. The times are simulated.
256 devices in a mesh: wide: 32 (over z_lo, x, core), narrow: 8 (over z_hi, y).
Axes of the slice: x: 4, y: 4, z: 8 (z_hi: 2, z_lo: 4; z = z_hi * 4 + z_lo), core: 2. Of those that a mesh axis runs over, the one named last changes fastest.
Arguments:
- stem: float32 [2, 1, 32, 256, 8, 256], P(None, None, 'wide', None, 'narrow'), may hold values from -6 to 6
- branch_pair: float32 [2, 2, 256, 256], P(None, None, ('wide', 'narrow')), may hold values from -0.25 to 0.25
- branch_last: float32 [2, 256, 256], P(None, 'narrow'), may hold values from -0.25 to 0.25
Outputs:
- absorbed: float32 [2, 1, 32, 256, 8, 256], P(None, None, 'wide', None, 'narrow')
All inputs are finite; a program needn't handle non-finite values.
Results may differ from a plain program's by a relative error of at most 0.000098.
Values sent between devices are 32-bit elements; how exact they have to be, the bound alone decides.
A program may use at most 64 MiB of HBM per device.

v0:
```python
import jax
import jax.numpy as jnp
from jax import lax
from jax.sharding import PartitionSpec as P

HIGHEST = lax.Precision.HIGHEST


def from_partner(value, axis, stride):
    return lax.ppermute(value, axis, [(i, i ^ 1 << stride) for i in range(lax.axis_size(axis))])


def complex_apply(form, branch, data):

    def single(matrix, values):
        return jnp.einsum(form, matrix, values, precision=HIGHEST)

    real_part = single(branch[0], data[0]) - single(branch[1], data[1])
    imag_part = single(branch[0], data[1]) + single(branch[1], data[0])
    return jnp.stack([real_part, imag_part])


def part_bit(values, position, stride, bit_flag):
    sizes = values.shape
    split_shape = (
        sizes[:position] + (sizes[position] // (2 * stride), 2, stride) + sizes[position + 1 :]
    )
    reshaped = values.reshape(split_shape)
    low_half = lax.index_in_dim(reshaped, 0, position + 1, keepdims=False)
    high_half = lax.index_in_dim(reshaped, 1, position + 1, keepdims=False)
    upper_flag = bit_flag == 1
    return (jnp.where(upper_flag, high_half, low_half), jnp.where(upper_flag, low_half, high_half))


def join_bit(kept_half, received, position, bit_flag, full_shape):
    upper_flag = bit_flag == 1
    low_half = jnp.where(upper_flag, received, kept_half)
    high_half = jnp.where(upper_flag, kept_half, received)
    return jnp.stack([low_half, high_half], axis=position + 1).reshape(full_shape)


def on_device(stem, branch_pair, branch_last):
    stem_rows = stem.shape[1]
    group_size = stem.shape[3]
    tail_size = stem.shape[5]
    wide_count = lax.axis_size("wide")
    narrow_count = lax.axis_size("narrow")
    flat_shape = (2, stem_rows, group_size, tail_size)

    def fetch_pair(number):
        return lax.all_gather(branch_pair[number], ("wide", "narrow"), axis=1, tiled=True)

    first_branch = fetch_pair(0)
    tail_branch = lax.all_gather(branch_last, "narrow", axis=1, tiled=True)
    current = stem.reshape(flat_shape)
    wide_place = lax.axis_index("wide")
    wide_stride = group_size // wide_count
    wide_bits = wide_count.bit_length() - 1
    for bit_index in range(wide_bits):
        bit_flag = wide_place >> bit_index & 1
        kept_half, sent_half = part_bit(current, 2, wide_stride * 2**bit_index, bit_flag)
        received = from_partner(sent_half, "wide", bit_index)
        current = join_bit(kept_half, received, 2, bit_flag, flat_shape)
    current = complex_apply("kj,rjh->rkh", first_branch, current)
    for bit_index in range(wide_bits):
        bit_flag = wide_place >> bit_index & 1
        kept_half, sent_half = part_bit(current, 2, wide_stride * 2**bit_index, bit_flag)
        received = from_partner(sent_half, "wide", bit_index)
        current = join_bit(kept_half, received, 2, bit_flag, flat_shape)
    narrow_place = lax.axis_index("narrow")
    narrow_stride = tail_size // narrow_count
    narrow_bits = narrow_count.bit_length() - 1
    for bit_index in range(narrow_bits):
        bit_flag = narrow_place >> bit_index & 1
        kept_half, sent_half = part_bit(current, 3, narrow_stride * 2**bit_index, bit_flag)
        received = from_partner(sent_half, "narrow", bit_index)
        current = join_bit(kept_half, received, 3, bit_flag, flat_shape)
    current = complex_apply("kj,rgj->rgk", tail_branch, current)
    for bit_index in range(narrow_bits):
        bit_flag = narrow_place >> bit_index & 1
        kept_half, sent_half = part_bit(current, 3, narrow_stride * 2**bit_index, bit_flag)
        received = from_partner(sent_half, "narrow", bit_index)
        current = join_bit(kept_half, received, 3, bit_flag, flat_shape)
    current = current.reshape(stem.shape)
    third_branch = fetch_pair(1)
    lower_three = group_size // (wide_count * narrow_count)
    spread = lax.all_to_all(
        lax.all_to_all(current, "wide", split_axis=3, concat_axis=2, tiled=True),
        "narrow",
        split_axis=3,
        concat_axis=4,
        tiled=True,
    )
    mixed = complex_apply("kj,rjh->rkh", third_branch, spread.reshape(flat_shape))
    mixed = mixed.reshape(2, stem_rows, wide_count, 1, lower_three, narrow_count, tail_size)
    returned = lax.all_to_all(
        lax.all_to_all(mixed, "wide", split_axis=2, concat_axis=3, tiled=True),
        "narrow",
        split_axis=5,
        concat_axis=4,
        tiled=True,
    )
    return returned.reshape(stem.shape)


def solution(mesh):
    in_specs = (
        P(None, None, "wide", None, "narrow", None),
        P(None, None, ("wide", "narrow"), None),
        P(None, "narrow", None),
    )
    out_specs = P(None, None, "wide", None, "narrow", None)
    return jax.shard_map(
        on_device, mesh=mesh, in_specs=in_specs, out_specs=out_specs, check_vma=False
    )
```

profile of v0, /device:TPU:1, one launch (start us, length us, event | category | flops | bytes accessed | tf_op | source)
XLA Modules:
  0.0 1737.6 jit_solution(9207599336118312875)
XLA Ops:
  0.0 1.1 copy.276
  1.1 3.3 collective-permute-start
  4.4 1.2 collective-permute-done
  5.8 0.1 collective-permute-start.1
  5.9 7.5 collective-permute-done.1
  13.6 1.1 collective-permute-start.2
  14.7 7.1 collective-permute-done.2
  22.0 0.1 collective-permute-start.3
  22.1 0.6 copy-done.1
  22.7 5.1 collective-permute-done.3
  28.0 1.7 collective-permute-start.4
  29.7 714.0 %all-gather = f32[1,2,256,256]{3,1,0,2:T(2,128)S(1)} all-gather(f32[1,2,1,256]{3,1,0,2:T(2,128)S(1)} %copy.288), channel_id=2, replica_groups=mesh['wide'=32,'narrow'=8] {'wide','narrow'}, dimensions={2}, use_global_device_ids=true | all-gather | bytes 526336 | tf_op jit(solution)/shard_map/all_gather | solution.py:51
  743.6 0.4 fusion.80
  744.2 0.4 fusion.32
  744.6 0.4 fusion.30
  745.0 0.4 convolution_subtract_fusion.2
  745.4 0.4 convolution_add_fusion.2
  745.9 0.1 collective-permute-start.5
  746.0 1.5 collective-permute-done.5
  747.7 11.7 collective-permute-start.6
  759.4 6.4 collective-permute-done.6
  766.0 2.7 collective-permute-start.7
  768.7 5.8 collective-permute-done.7
  774.7 23.4 %collective-permute-start.8 = (f32[2,1,2,64,256]{4,3,2,0,1:T(8,128)S(1)}, f32[2,1,2,64,256]{4,3,2,0,1:T(8,128)S(1)}, u32[]{:S(2)}, u32[]{:S(2)}) collective-permute-start(f32[2,1,2,64,256]{4,3,2,0,1:T(8,128)S(1)} %select_bitcast_fusion.3), channel_id=1, source_target_pairs={{0,64},{8,72},{16,80},{24,88},{32,96},{40,104},{48,112},{56,120},{... | collective-permute-start | bytes 786440 | tf_op jit(solution)/shard_map/ppermute | solution.py:10
  798.2 4.5 collective-permute-done.8
  802.8 0.6 collective-permute-start.9
  803.4 13.3 collective-permute-done.9
  816.8 0.2 copy.244
  817.0 0.3 fusion.6
  817.3 0.5 collective-permute-start.10
  817.8 6.1 collective-permute-done.10
  823.9 0.5 fusion.2
  824.5 0.7 pad_maximum_fusion.9
  825.3 6.7 collective-permute-done.11
  832.2 0.9 collective-permute-start.12
  833.1 47.1 %all_gather.10 = f32[2,256,256]{2,1,0:T(8,128)S(1)} all-gather(f32[2,32,256]{2,1,0:T(8,128)S(1)} %copy-done), channel_id=1, replica_groups=mesh['wide'=32,'narrow'=8] {'narrow'}, dimensions={1}, use_global_device_ids=true | all-gather | bytes 589824 | tf_op jit(solution)/shard_map/all_gather | solution.py:54
  880.4 0.4 fusion.66
  880.8 0.4 fusion.67
  881.2 0.4 convolution_add_fusion.1
  881.6 0.4 convolution_subtract_fusion.1
  882.0 0.3 copy_dynamic-update-slice_fusion.1
  882.3 0.3 copy_dynamic-update-slice_fusion
  882.5 0.3 fusion.8
  882.9 5.2 collective-permute-done.13
  888.1 0.5 fusion.4
  888.6 0.7 pad_maximum_fusion.11
  889.4 8.0 collective-permute-done.14
  897.7 2.9 collective-permute-start.15
  900.5 6.3 collective-permute-done.15
  907.0 0.2 copy.262
  907.3 34.9 %all_to_all.42 = f32[2,1,1,256,1,256]{5,0,4,2,1,3:T(2,128)S(1)} all-to-all(f32[2,1,1,256,1,256]{5,0,4,2,1,3:T(2,128)S(1)} %copy.262), channel_id=1, replica_groups=mesh['wide'=32,'narrow'=8] {'wide'}, dimensions={3} | all-to-all | bytes 1048576 | tf_op jit(solution)/shard_map/all_to_all | solution.py:88
  942.2 1.1 copy.264
  943.3 5.5 all-to-all-start.1
  948.8 717.2 %all-gather.1 = f32[1,2,256,256]{3,1,0,2:T(2,128)S(1)} all-gather(f32[1,2,1,256]{3,1,0,2:T(2,128)S(1)} %copy.301), channel_id=3, replica_groups=mesh['wide'=32,'narrow'=8] {'wide','narrow'}, dimensions={2}, use_global_device_ids=true | all-gather | bytes 526336 | tf_op jit(solution)/shard_map/all_gather | solution.py:51
  1666.0 0.4 fusion.78
  1666.5 0.5 fusion.26
  1667.0 0.5 fusion.24
  1667.6 0.5 fusion.1
  1668.1 0.5 fusion
  1668.7 49.0 %all_to_all.43 = f32[2,1,32,1,1,8,256]{6,5,4,3,1,0,2:T(8,128)S(1)} all-to-all(f32[2,1,32,1,1,8,256]{6,5,4,3,1,0,2:T(8,128)S(1)} %pad_maximum_fusion.14), channel_id=1, replica_groups=mesh['wide'=32,'narrow'=8] {'wide'}, dimensions={2} | all-to-all | bytes 1048576 | tf_op jit(solution)/shard_map/all_to_all | solution.py:97
  1717.7 0.3 copy.270
  1718.0 18.0 %all_to_all.44 = f32[2,1,1,32,1,8,256]{6,3,0,4,2,1,5:T(8,128)S(1)} all-to-all(f32[2,1,1,32,1,8,256]{6,3,0,4,2,1,5:T(8,128)S(1)} %copy.270), channel_id=1, replica_groups=mesh['wide'=32,'narrow'=8] {'narrow'}, dimensions={5} | all-to-all | bytes 1048576 | tf_op jit(solution)/shard_map/all_to_all | solution.py:96
  1736.0 0.3 copy.349
  1736.3 1.3 copy.272
  (69 shorter events, 2.7 us)
Async XLA Ops:
  1.1 4.5 collective-permute-start
  5.8 7.6 collective-permute-start.1
  13.6 8.2 collective-permute-start.2
  22.0 0.7 copy-start.1
  22.0 5.8 collective-permute-start.3
  28.0 716.1 %collective-permute-start.4 = (f32[2,1,1,128,256]{4,3,0,2,1:T(8,128)S(1)}, f32[2,1,1,128,256]{4,3,0,2,1:T(8,128)S(1)}, u32[]{:S(2)}, u32[]{:S(2)}) collective-permute-start(f32[2,1,1,128,256]{4,3,0,2,1:T(8,128)S(1)} %fusion.17), channel_id=1, source_target_pairs={{0,128},{8,136},{16,144},{24,152},{32,160},{40,168},{48,176},{56,1... | collective-permute-start | bytes 786440 | tf_op jit(solution)/shard_map/ppermute | solution.py:10
  745.9 1.6 collective-permute-start.5
  747.7 18.1 %collective-permute-start.6 = (f32[2,1,8,16,256]{4,3,2,0,1:T(8,128)S(1)}, f32[2,1,8,16,256]{4,3,2,0,1:T(8,128)S(1)}, u32[]{:S(2)}, u32[]{:S(2)}) collective-permute-start(f32[2,1,8,16,256]{4,3,2,0,1:T(8,128)S(1)} %select_bitcast_fusion.5), channel_id=1, source_target_pairs={{0,16},{8,24},{16,0},{24,8},{32,48},{40,56},{48,32},{56,40},{64,80... | collective-permute-start | bytes 786440 | tf_op jit(solution)/shard_map/ppermute | solution.py:10
  766.0 8.5 collective-permute-start.7
  774.7 27.9 %collective-permute-start.8 = (f32[2,1,2,64,256]{4,3,2,0,1:T(8,128)S(1)}, f32[2,1,2,64,256]{4,3,2,0,1:T(8,128)S(1)}, u32[]{:S(2)}, u32[]{:S(2)}) collective-permute-start(f32[2,1,2,64,256]{4,3,2,0,1:T(8,128)S(1)} %select_bitcast_fusion.3), channel_id=1, source_target_pairs={{0,64},{8,72},{16,80},{24,88},{32,96},{40,104},{48,112},{56,120},{... | collective-permute-start | bytes 786440 | tf_op jit(solution)/shard_map/ppermute | solution.py:10
  802.8 13.9 collective-permute-start.9
  817.3 6.6 collective-permute-start.10
  825.2 6.8 collective-permute-start.11
  832.2 0.9 copy-start
  832.2 48.0 %collective-permute-start.12 = (f32[2,1,256,1,128]{2,4,0,3,1:T(8,128)S(1)}, f32[2,1,256,1,128]{2,4,0,3,1:T(8,128)S(1)}, u32[]{:S(2)}, u32[]{:S(2)}) collective-permute-start(f32[2,1,256,1,128]{2,4,0,3,1:T(8,128)S(1)} %fusion.15), channel_id=1, source_target_pairs={{0,4},{1,5},{2,6},{3,7},{4,0},{5,1},{6,2},{7,3},{8,12},{9,13},{10,... | collective-permute-start | bytes 786440 | tf_op jit(solution)/shard_map/ppermute | solution.py:10
  882.8 5.3 collective-permute-start.13
  889.3 8.1 collective-permute-start.14
  897.7 9.2 collective-permute-start.15
  943.3 723.1 %all-to-all-start.1 = ((f32[2,1,32,8,1,256]{5,2,0,4,1,3:T(8,128)}), f32[2,1,32,8,1,256]{5,2,0,4,1,3:T(8,128)S(1)}, u32[]{:S(2)}, u32[]{:S(2)}) async-start(f32[2,1,32,8,1,256]{5,2,0,4,1,3:T(8,128)} %copy.264), calls=%async_computation.1 | async-start | bytes 1048576 | tf_op jit(solution)/shard_map/all_to_all | solution.py:87
where the time goes:
time: 1740 us
  blocking collectives  1580 us (91%)
  waiting for transfers between devices  84.8 us (5%)
  starting transfers between devices  54.8 us (3%)
    all_gather x2, blocking collectives, fetch_pair(): lax.all_gather(branch_pair[number], ('wide', 'narrow'), axis=1, tiled=True)  1430 us
    ppermute x16, waiting for transfers between devices, from_partner(): lax.ppermute(value, axis, [(i, i ^ 1 << stride) for i in range(lax.axis_s...  84.8 us
    ppermute x16, starting transfers between devices, from_partner(): lax.ppermute(value, axis, [(i, i ^ 1 << stride) for i in range(lax.axis_s...  49.3 us
    all_to_all x1, blocking collectives, on_device(): lax.all_to_all(mixed, 'wide', split_axis=2, concat_axis=3, tiled=True)  49 us
    all_gather x1, blocking collectives, on_device(): tail_branch = lax.all_gather(branch_last, 'narrow', axis=1, tiled=True)  47.1 us
    all_to_all x1, blocking collectives, on_device(): lax.all_to_all(current, 'wide', split_axis=3, concat_axis=2, tiled=True)  34.9 us
  transfers between devices with their start and end apart: 17, of which 14 were waited for; matrix products, arithmetic and copies ran while one was open for 0% of the time, Pallas kernels for 0%

commit v1 on v0

v1 whole, which is shorter than its diff:
```python
import jax
import jax.numpy as jnp
from jax import lax
from jax.sharding import PartitionSpec as P

PRECISION = lax.Precision.HIGH
BOTH = ("wide", "narrow")


def multiply(form, branch, data):

    def single(matrix, values):
        return jnp.einsum(form, matrix, values, precision=PRECISION)

    real_part = single(branch[0], data[0]) - single(branch[1], data[1])
    imag_part = single(branch[0], data[1]) + single(branch[1], data[0])
    return jnp.stack([real_part, imag_part])


def on_device(stem, branch_pair, branch_last):
    group_size = stem.shape[3]
    tail_size = stem.shape[5]
    wide_count = lax.axis_size("wide")
    narrow_count = lax.axis_size("narrow")
    devices = wide_count * narrow_count
    g_low = group_size // wide_count
    t_low = tail_size // narrow_count

    pair = lax.all_gather(branch_pair, BOTH, axis=2, tiled=True)
    tail = lax.all_gather(branch_last, "narrow", axis=1, tiled=True)

    blocks = stem.reshape(2, wide_count, g_low, narrow_count, t_low)
    blocks = blocks.transpose(1, 3, 0, 2, 4).reshape(devices, -1)
    blocks = lax.all_to_all(blocks, BOTH, split_axis=0, concat_axis=0, tiled=True)
    blocks = blocks.reshape(wide_count, narrow_count, 2, g_low, t_low)
    current = blocks.transpose(2, 0, 3, 1, 4).reshape(2, wide_count * g_low, narrow_count * t_low)
    current = multiply("kj,jh->kh", pair[0], current)
    current = multiply("kj,gj->gk", tail, current)
    current = current.reshape(2, wide_count, g_low, narrow_count, t_low)
    current = current.transpose(0, 1, 3, 2, 4).reshape(2, devices, g_low * t_low)
    current = multiply("kj,jh->kh", pair[1], current)
    blocks = current.transpose(1, 0, 2).reshape(devices, -1)
    blocks = lax.all_to_all(blocks, BOTH, split_axis=0, concat_axis=0, tiled=True)
    blocks = blocks.reshape(wide_count, narrow_count, 2, g_low, t_low)
    return blocks.transpose(2, 0, 3, 1, 4).reshape(stem.shape)


def solution(mesh):
    in_specs = (
        P(None, None, "wide", None, "narrow", None),
        P(None, None, ("wide", "narrow"), None),
        P(None, "narrow", None),
    )
    out_specs = P(None, None, "wide", None, "narrow", None)
    return jax.shard_map(
        on_device, mesh=mesh, in_specs=in_specs, out_specs=out_specs, check_vma=False
    )
```

time: 1740 us -> 600 us (0.34)
  blocking collectives: 1580 us -> 77.8 us
  waiting for transfers between devices: 84.8 us -> 462 us
  starting transfers between devices: 54.8 us -> 15.7 us
    all_gather x3 -> x1, blocking collectives: 1480 us -> 48.9 us  [on_device(): tail = lax.all_gather(branch_last, 'narrow', axis=1, tiled=True)]
    all_gather x0 -> x1, waiting for transfers between devices: none -> 462 us  [on_device(): pair = lax.all_gather(branch_pair, BOTH, axis=2, tiled=True)]
    ppermute x16 -> x0, waiting for transfers between devices: 84.8 us -> none  [from_partner(): lax.ppermute(value, axis, [(i, i ^ 1 << stride) for i in range(lax.axis_s...]
    all_to_all x3 -> x1, blocking collectives: 102 us -> 28.9 us  [on_device(): lax.all_to_all(blocks, BOTH, split_axis=0, concat_axis=0, tiled=True)]
    ppermute x16 -> x0, starting transfers between devices: 49.3 us -> none  [from_partner(): lax.ppermute(value, axis, [(i, i ^ 1 << stride) for i in range(lax.axis_s...]
  transfers between devices with their start and end apart: 17 -> 2, of which waited for: 14 -> 1; matrix products, arithmetic and copies ran while one was open for 0% -> 1% of each run, Pallas kernels for 0% -> 0%
where the time goes in v1:
time: 600 us; the launch traced here: 599 us
  waiting for transfers between devices  462 us (77%)
  blocking collectives  77.8 us (13%)
  local copies, waits for them, and re-layouts  20.7 us (3%)
  starting transfers between devices  15.7 us (3%)
  between operations  13.6 us (2%)
    all_gather x1, waiting for transfers between devices, on_device(): pair = lax.all_gather(branch_pair, BOTH, axis=2, tiled=True)  462 us
    all_gather x1, blocking collectives, on_device(): tail = lax.all_gather(branch_last, 'narrow', axis=1, tiled=True)  48.9 us
    all_to_all x1, blocking collectives, on_device(): lax.all_to_all(blocks, BOTH, split_axis=0, concat_axis=0, tiled=True)  28.9 us
    all_to_all x1, starting transfers between devices, on_device(): lax.all_to_all(blocks, BOTH, split_axis=0, concat_axis=0, tiled=True)  15.7 us
  transfers between devices with their start and end apart: 2, of which 1 were waited for; matrix products, arithmetic and copies ran while one was open for 1% of the time, Pallas kernels for 0%

profile of v1, /device:TPU:1, one launch (start us, length us, event | category | flops | bytes accessed | tf_op | source)
XLA Modules:
  0.0 599.3 jit_solution(810046756343872462)
XLA Ops:
  6.5 0.0 all-gather.2.cloned.1.call-start
  6.5 1.3 copy.17
  7.8 0.0 all-gather.2.cloned.1.call-update
  7.8 2.3 reduce
  10.1 0.5 reshape.45
  10.6 1.7 copy.65
  12.3 0.0 copy-start.1
  12.3 3.2 all_to_all.16
  15.5 15.7 %all-to-all-start = ((f32[256,1,512]{2,1,0:T(1,128)}), f32[256,1,512]{2,1,0:T(1,128)S(1)}, u32[]{:S(2)}, u32[]{:S(2)}) async-start(f32[256,1,512]{2,1,0:T(1,128)} %all_to_all.16), calls=%async_computation | async-start | bytes 1048576 | tf_op jit(solution)/shard_map/all_to_all | solution.py:34
  31.2 0.0 copy-done.1
  31.2 48.9 %all_gather.7 = f32[2,256,256]{2,1,0:T(8,128)S(1)} all-gather(f32[2,32,256]{2,1,0:T(8,128)S(1)} %copy-done.1), channel_id=1, replica_groups=mesh['wide'=32,'narrow'=8] {'narrow'}, dimensions={1}, use_global_device_ids=true | all-gather | bytes 589824 | tf_op jit(solution)/shard_map/all_gather | solution.py:30
  80.1 0.0 all-to-all-done
  80.1 1.2 reduce.1
  81.3 0.5 reshape.46
  81.9 0.7 copy.64
  82.6 0.2 fusion.25
  82.8 0.3 squeeze.45
  83.1 0.3 squeeze.21
  83.5 461.6 %all-gather.2.cloned.1.call-done = f32[2,2,256,256]{3,1,0,2:T(2,128)} async-done(((f32[2,2,1,256]{3,1,0,2:T(2,128)}), f32[2,2,256,256]{3,1,0,2:T(2,128)}) %all-gather.2.cloned.1.call-update) | async-done | bytes 1048592 | tf_op jit(solution)/shard_map/all_gather | solution.py:29
  545.1 3.2 fusion.26
  548.3 0.3 fusion.10
  548.6 0.3 fusion.12
  548.9 0.3 convolution_add_fusion.2
  549.2 0.3 convolution_subtract_fusion.2
  549.4 0.3 fusion.14
  549.8 0.3 fusion.15
  550.1 0.3 convolution_add_fusion.1
  550.5 0.3 stack.19
  550.8 0.2 copy.22
  551.0 1.0 convolution_subtract_fusion.1
  552.0 1.2 stack.18
  553.2 0.2 copy.21
  553.4 0.3 maximum_bitcast_fusion
  553.7 0.2 fusion.24
  553.9 0.0 copy-start
  553.9 0.3 squeeze.50
  554.3 0.3 squeeze.48
  554.6 0.4 fusion.4
  555.0 0.4 fusion.6
  555.4 0.0 copy-done
  555.4 0.4 fusion
  555.8 0.4 fusion.1
  556.2 0.4 copy.23
  556.6 28.9 %all_to_all.19 = f32[256,1,512]{2,1,0:T(1,128)S(1)} all-to-all(f32[256,1,512]{2,1,0:T(1,128)S(1)} %copy.23), channel_id=1, replica_groups=mesh['wide'=32,'narrow'=8] {'wide','narrow'}, dimensions={0} | all-to-all | bytes 1048576 | tf_op jit(solution)/shard_map/all_to_all | solution.py:43
  585.5 1.2 reduce.2
  586.8 0.5 reshape.47
  587.3 2.0 copy.24
  589.3 3.1 reshape.49
  (1 shorter events, 0.0 us)
Async XLA Ops:
  6.5 538.6 %all-gather.2.cloned.1.call-start = ((), (), s32[]{:S(2)}) async-start(), calls=%async_computation.2 | async-start | bytes 1052672 | tf_op jit(solution)/shard_map/all_gather | solution.py:29
  12.3 18.8 %copy-start.1 = (f32[2,32,256]{2,1,0:T(8,128)S(1)}, f32[2,32,256]{2,1,0:T(8,128)}, u32[]{:S(2)}) copy-start(f32[2,32,256]{2,1,0:T(8,128)} %param.5) | copy-start | bytes 196612
  15.5 64.6 %all-to-all-start = ((f32[256,1,512]{2,1,0:T(1,128)}), f32[256,1,512]{2,1,0:T(1,128)S(1)}, u32[]{:S(2)}, u32[]{:S(2)}) async-start(f32[256,1,512]{2,1,0:T(1,128)} %all_to_all.16), calls=%async_computation | async-start | bytes 1048576 | tf_op jit(solution)/shard_map/all_to_all | solution.py:34
  553.9 1.4 copy-start
Sparse Core Ops, SparseCore 0:
  9.1 535.9 all-gather.1

commit v2 on v1

v2 whole, which is shorter than its diff:
```python
import functools

import jax
import jax.numpy as jnp
from jax import lax
from jax.experimental import pallas as pl
from jax.experimental.pallas import tpu as pltpu
from jax.sharding import PartitionSpec as P

MESH = pl.DeviceIdType.MESH
F32 = jnp.float32
BF16 = jnp.bfloat16


def rows(start, count=8):
    return pl.ds(pl.multiple_of(start, 8), count)


def device(z, y, x, core):
    return ((z & 3) * 8 + x * 2 + core, (z >> 2) * 4 + y)


def swap_blocks(tiles):
    lane = lax.broadcasted_iota(jnp.int32, tiles[0].shape, 1)
    low64 = lane < 64
    low32 = (lane & 32) == 0

    def halves(a, b):
        r = pltpu.roll(jnp.where(low64, b, a), 64, 1)
        return jnp.where(low64, a, r), jnp.where(low64, r, b)

    def quarters(a, b):
        return (
            jnp.where(low32, a, pltpu.roll(b, 32, 1)),
            jnp.where(low32, pltpu.roll(a, 96, 1), b),
        )

    a0, a2 = halves(tiles[0], tiles[2])
    a1, a3 = halves(tiles[1], tiles[3])
    return (*quarters(a0, a1), *quarters(a2, a3))


def split(values):
    high = values.astype(BF16)
    return high, (values - high.astype(F32)).astype(BF16)


def dot(a, b):
    return jnp.dot(a, b, preferred_element_type=F32)


def product(ar, ai, br, bi):
    def left(v):
        return jnp.concatenate([v[0], v[0], v[1]], axis=1)

    def right(v):
        return jnp.concatenate([v[0], v[1], v[0]], axis=0)

    lr, li, rr, ri = left(ar), left(ai), right(br), right(bi)
    return dot(lr, rr) - dot(li, ri), dot(lr, ri) + dot(li, rr)


def kernel(
    stem,
    pair,
    tail,
    out,
    xr,
    sent,
    got,
    ga,
    gb,
    wh,
    wl,
    x1,
    y2,
    zz,
    back,
    home,
    final,
    plane_sem,
    local_sem,
    pair_send,
    pair_recv,
    z_send,
    z_recv,
    ring_send,
    ring_recv,
    core_send,
    core_recv,
    go_send,
    go_recv,
    back_send,
    back_recv,
    out_send,
    out_recv,
):
    wide, narrow = lax.axis_index("wide"), lax.axis_index("narrow")
    core, x = wide & 1, (wide >> 1) & 3
    z, y = (narrow >> 2) * 4 + (wide >> 3), narrow & 3
    other = 1 - core
    sibling = device(z, y, x, other)

    def at_z(d):
        return (z + d) & 7

    def at_x(d):
        return (x + d) & 3

    def at_y(d):
        return (y + d) & 3

    def own_half(c):
        return pltpu.make_async_copy(
            stem.at[rows(c * 512 + core * 256, 256)],
            xr.at[rows(core * 512 + c * 256, 256)],
            local_sem.at[c],
        )

    for c in range(2):
        own_half(c).start()

    barrier = pltpu.get_barrier_semaphore()
    pl.semaphore_signal(barrier, inc=1, device_id=sibling, device_id_type=MESH)
    for d in range(1, 8):
        pl.semaphore_signal(barrier, inc=1, device_id=device(at_z(d), y, x, core), device_id_type=MESH)
    for d in range(1, 16):
        pl.semaphore_signal(
            barrier, inc=1, device_id=device(z, at_y(d // 4), at_x(d % 4), core), device_id_type=MESH
        )

    slot_a = ((core * 4 + y) * 8 + z) * 4 + x
    slot_b = ((core * 4 + x) * 8 + z) * 4 + y
    ga[rows(slot_a * 8), :] = pair[...]
    line = lax.broadcasted_iota(jnp.int32, (8, 128), 0)
    pieces = []
    for c in range(2):
        for h in range(2):
            tile = tail[c, rows((z & 3) * 8), h * 128 : h * 128 + 128]
            pieces.append(jnp.sum(jnp.where(line == core * 4 + x, tile, 0.0), axis=0, keepdims=True))
    gb[rows(slot_b * 8), :] = jnp.concatenate([*pieces, jnp.zeros((4, 128), F32)], axis=0)

    pl.semaphore_wait(barrier, 23)

    for d in range(1, 8):
        pl.semaphore_signal(plane_sem, inc=1, device_id=device(at_z(d), y, x, core), device_id_type=MESH)

    def half_across(c):
        return pltpu.make_async_remote_copy(
            stem.at[rows(c * 512 + other * 256, 256)],
            xr.at[rows(core * 512 + c * 256, 256)],
            pair_send.at[c],
            pair_recv.at[c],
            device_id=sibling,
            device_id_type=MESH,
        )

    for c in range(2):
        half_across(c).start()

    def along_z(buffer, which, slot, d):
        return pltpu.make_async_remote_copy(
            buffer.at[rows(slot * 8)],
            buffer.at[rows(slot * 8)],
            z_send.at[which],
            z_recv.at[which],
            device_id=device(at_z(d), y, x, core),
            device_id_type=MESH,
        )

    for d in (4, 3, 5, 2, 6, 1, 7):
        along_z(ga, 0, slot_a, d).start()
        along_z(gb, 1, slot_b, d).start()

    for c in range(2):
        own_half(c).wait()
    for c in range(2):
        half_across(c).wait()
    pl.semaphore_wait(plane_sem, 7)

    def block_ax(p):
        return lambda lo, n: ga.reshape(2, 4, 8, 4, 8, 128).at[core, y, pl.ds(lo, n), p]

    def block_by(p):
        return lambda lo, n: gb.reshape(2, 4, 8, 4, 8, 128).at[core, x, pl.ds(lo, n), p]

    def block_ay(p):
        return lambda lo, n: ga.reshape(2, 4, 8, 4, 8, 128).at[core, p, pl.ds(lo, n)]

    def block_bx(p):
        return lambda lo, n: gb.reshape(2, 4, 8, 4, 8, 128).at[core, p, pl.ds(lo, n)]

    def on_x(d):
        return at_x(d), device(z, y, at_x(d), core)

    def on_y(d):
        return at_y(d), device(z, at_y(d), x, core)

    def ring_copy(number, block, step, place, lo, n):
        holder = place(0)[0] if step < 2 else place(-1 if step == 2 else 1)[0]
        ref = block(holder)(lo, n)
        return pltpu.make_async_remote_copy(
            ref,
            ref,
            ring_send.at[number, step],
            ring_recv.at[number, step],
            device_id=place(1 if step in (0, 2) else -1)[1],
            device_id_type=MESH,
        )

    def ring(number, block, place):
        copies = [
            ring_copy(number, block, 0, place, 0, 8),
            ring_copy(number, block, 1, place, 0, 8),
            ring_copy(number, block, 2, place, 0, 4),
            ring_copy(number, block, 3, place, 4, 4),
        ]

        def start():
            copies[0].start()
            copies[1].start()

        def forward():
            copies[0].wait_recv()
            copies[2].start()
            copies[1].wait_recv()
            copies[3].start()

        def finish():
            copies[2].wait_recv()
            copies[3].wait_recv()

        def drain():
            for copy in copies:
                copy.wait_send()

        return start, forward, finish, drain

    rings = [
        ring(0, block_ax, on_x),
        ring(1, block_by, on_y),
        ring(2, block_ay, on_y),
        ring(3, block_bx, on_x),
    ]

    here = (((z & 3) * 4 + x) * 2 + (z >> 2)) * 4 + y

    def shuffle_group(number, zt, xt):
        base = ((zt & 3) * 4 + xt) * 16 + (zt >> 2)
        tiles = [xr[pl.ds(i * 256 + base, 8, stride=2), :] for i in range(4)]
        for j, tile in enumerate(swap_blocks(tiles)):
            sent[rows((number * 4 + j) * 8), :] = tile

    def send_tile(number, zt, yt, xt):
        pltpu.make_async_remote_copy(
            sent.at[rows((number * 4 + yt) * 8)],
            got.at[rows(here * 8)],
            go_send,
            go_recv,
            device_id=device(zt, yt, xt, core),
            device_id_type=MESH,
        ).start()

    def send_groups(dx, dzs):
        for dz in dzs:
            zt, xt = at_z(dz), at_x(dx)
            number = dx * 8 + dz
            shuffle_group(number, zt, xt)
            for dy in range(4):
                send_tile(number, zt, at_y(dy), xt)

    send_groups(0, (4, 3, 5, 2, 6, 1, 7))
    part = rows(0, 56)
    for which, buffer in ((0, ga), (1, gb)):
        pltpu.make_async_copy(buffer.at[part], buffer.at[part], z_recv.at[which]).wait()
    rings[0][0]()
    rings[1][0]()
    send_groups(1, (4, 3, 5, 2, 6, 1, 7, 0))
    rings[0][1]()
    rings[1][1]()
    send_groups(2, (4, 3, 5, 2, 6, 1, 7, 0))
    rings[0][2]()
    rings[1][2]()
    rings[2][0]()
    rings[3][0]()
    send_groups(3, (4, 3, 5, 2, 6, 1, 7, 0))
    shuffle_group(0, z, x)
    for dy in range(1, 4):
        send_tile(0, z, at_y(dy), x)
    got[rows(here * 8), :] = sent[rows(y * 8), :]
    rings[2][1]()
    rings[3][1]()
    rings[2][2]()
    rings[3][2]()

    def core_copy(which, buffer):
        ref = buffer.at[rows(core * 1024, 1024)]
        return pltpu.make_async_remote_copy(
            ref, ref, core_send.at[which], core_recv.at[which], device_id=sibling, device_id_type=MESH
        )

    core_copy(0, ga).start()
    core_copy(1, gb).start()
    core_copy(0, ga).wait_recv()
    core_copy(1, gb).wait_recv()

    def weights(step, c):
        halves = []
        for h in range(2):
            k = step * 4 + c * 2 + h
            halves.append(jnp.concatenate([ga[pl.ds(i * 64 + k, 8, stride=8), :] for i in range(32)], axis=0))
        return jnp.concatenate(halves, axis=1)

    def tail_weights(c):
        halves = []
        for h in range(2):
            k = c * 2 + h
            blocks = []
            for i in range(32):
                zi, yi = (i // 16) * 4 + i % 4, (i // 4) % 4
                blocks.append(gb[pl.ds((zi * 4 + yi) * 8 + k, 8, stride=256), :])
            halves.append(jnp.concatenate(blocks, axis=0))
        return jnp.concatenate(halves, axis=1)

    for c in range(2):
        for step in range(2):
            wh[step, c], wl[step, c] = split(weights(step, c))
        wh[2, c], wl[2, c] = split(tail_weights(c).T)

    part = rows(0, 127 * 8)
    pltpu.make_async_copy(got.at[part], got.at[part], go_recv).wait()

    @pl.loop(0, 16)
    def _(i):
        for h in range(2):
            tiles = [got[rows((i * 8 + h * 4 + j) * 8), :] for j in range(4)]
            for k, tile in enumerate(swap_blocks(tiles)):
                x1[k % 2, rows(i * 16 + (k // 2) * 8), h * 128 : h * 128 + 128] = tile

    def weight(number, c):
        return wh[number, c], wl[number, c]

    first = product(weight(0, 0), weight(0, 1), split(x1[0]), split(x1[1]))
    second = product(split(first[0]), split(first[1]), weight(2, 0), weight(2, 1))
    y2[0] = second[0]
    y2[1] = second[1]
    for c in range(2):
        for k in range(2):
            for h in range(2):
                for vh in range(2):
                    for jb in range(2):
                        tiles = [
                            y2[c, rows(k * 128 + j * 32 + h * 16 + jb * 8), vh * 128 : vh * 128 + 128] for j in range(4)
                        ]
                        for j, tile in enumerate(swap_blocks(tiles)):
                            zz[c * 2 + h, pl.ds(jb * 128 + k * 8 + vh * 4 + j, 8, stride=16), :] = tile

    def contracted(c):
        return split(jnp.concatenate([zz[c * 2], zz[c * 2 + 1]], axis=1))

    third = product(weight(1, 0), weight(1, 1), contracted(0), contracted(1))
    for c in range(2):
        for k in range(2):
            for h in range(2):
                for i in range(16):
                    back[pl.ds(i * 64 + h * 4 + k * 2 + c, 8, stride=8), :] = third[c][
                        k * 128 + i * 8 : k * 128 + i * 8 + 8, h * 128 : h * 128 + 128
                    ]

    there = (z * 4 + x) * 4 + y

    def send_back(zt, yt, xt):
        pltpu.make_async_remote_copy(
            back.at[rows(((yt * 8 + zt) * 4 + xt) * 8)],
            home.at[rows(there * 8)],
            back_send,
            back_recv,
            device_id=device(zt, yt, xt, core),
            device_id_type=MESH,
        ).start()

    @pl.loop(0, 16)
    def _(i):
        for dz in (4, 3, 5, 2, 6, 1, 7):
            send_back(at_z(dz), at_y(i & 3), at_x(i >> 2))

        @pl.when(i > 0)
        def _():
            send_back(z, at_y(i & 3), at_x(i >> 2))

    home[rows(there * 8), :] = back[rows(((y * 8 + z) * 4 + x) * 8), :]
    part = rows(0, 127 * 8)
    pltpu.make_async_copy(home.at[part], home.at[part], back_recv).wait()

    @pl.loop(0, 16)
    def _(i):
        for h in range(2):
            group = h * 16 + i
            tiles = [home[rows((group * 4 + j) * 8), :] for j in range(4)]
            for j, tile in enumerate(swap_blocks(tiles)):
                for gh in range(2):
                    final[pl.ds(i * 16 + (gh * 4 + j) * 2 + h, 4, stride=256), :] = tile[gh * 4 : gh * 4 + 4]

    def out_here(c):
        return pltpu.make_async_copy(
            final.at[rows(core * 512 + c * 256, 256)], out.at[rows(c * 512 + core * 256, 256)], local_sem.at[c]
        )

    def out_across(c):
        return pltpu.make_async_remote_copy(
            final.at[rows(other * 512 + c * 256, 256)],
            out.at[rows(c * 512 + core * 256, 256)],
            out_send.at[c],
            out_recv.at[c],
            device_id=sibling,
            device_id_type=MESH,
        )

    for c in range(2):
        out_across(c).start()
        out_here(c).start()

    for which, buffer in ((0, ga), (1, gb)):
        core_copy(which, buffer).wait_send()
        pltpu.make_async_copy(buffer.at[rows(0, 56)], buffer.at[rows(0, 56)], z_send.at[which]).wait()
    for one in rings:
        one[3]()
    pltpu.make_async_copy(sent.at[part], sent.at[part], go_send).wait()
    pltpu.make_async_copy(back.at[part], back.at[part], back_send).wait()
    for c in range(2):
        out_here(c).wait()
        out_across(c).wait()


def on_device(stem, branch_pair, branch_last):
    dma = pltpu.SemaphoreType.DMA
    whole = pltpu.VMEM((1024, 128), F32)
    result = pl.pallas_call(
        kernel,
        out_shape=jax.ShapeDtypeStruct((1024, 128), F32),
        in_specs=[
            pl.BlockSpec(memory_space=pl.ANY),
            pl.BlockSpec(memory_space=pltpu.VMEM),
            pl.BlockSpec(memory_space=pltpu.VMEM),
        ],
        out_specs=pl.BlockSpec(memory_space=pl.ANY),
        scratch_shapes=[
            whole,
            whole,
            whole,
            pltpu.VMEM((2048, 128), F32),
            pltpu.VMEM((2048, 128), F32),
            pltpu.VMEM((3, 2, 256, 256), BF16),
            pltpu.VMEM((3, 2, 256, 256), BF16),
            pltpu.VMEM((2, 256, 256), F32),
            pltpu.VMEM((2, 256, 256), F32),
            pltpu.VMEM((4, 256, 128), F32),
            whole,
            whole,
            whole,
            pltpu.SemaphoreType.REGULAR,
            dma((2,)),
            dma((2,)),
            dma((2,)),
            dma((2,)),
            dma((2,)),
            dma((4, 4)),
            dma((4, 4)),
            dma((2,)),
            dma((2,)),
            dma,
            dma,
            dma,
            dma,
            dma((2,)),
            dma((2,)),
        ],
        compiler_params=pltpu.CompilerParams(collective_id=0, has_side_effects=True, vmem_limit_bytes=40 << 20),
        name="absorb",
    )(stem.reshape(1024, 128), branch_pair.reshape(8, 128), branch_last)
    return result.reshape(stem.shape)


def solution(mesh):
    in_specs = (
        P(None, None, "wide", None, "narrow", None),
        P(None, None, ("wide", "narrow"), None),
        P(None, "narrow", None),
    )
    out_specs = P(None, None, "wide", None, "narrow", None)
    return jax.shard_map(on_device, mesh=mesh, in_specs=in_specs, out_specs=out_specs, check_vma=False)
```

time: 600 us -> 62.7 us (0.10)
  waiting for transfers between devices: 462 us -> 0 us
  blocking collectives: 77.8 us -> 0 us
  Pallas kernels: 0 us -> 59.1 us
  local copies, waits for them, and re-layouts: 20.7 us -> 3.36 us
  starting transfers between devices: 15.7 us -> 0 us
  between operations: 13.6 us -> 0.01 us
    all_gather x1 -> x0, waiting for transfers between devices: 462 us -> none  [on_device(): pair = lax.all_gather(branch_pair, BOTH, axis=2, tiled=True)]
    pallas_call x0 -> x1, Pallas kernels: none -> 59.1 us  [on_device(): pl.pallas_call(kernel, out_shape=jax.ShapeDtypeStruct((1024, 128), F32),...]
    all_gather x1 -> x0, blocking collectives: 48.9 us -> none  [on_device(): tail = lax.all_gather(branch_last, 'narrow', axis=1, tiled=True)]
    all_to_all x1 -> x0, blocking collectives: 28.9 us -> none  [on_device(): lax.all_to_all(blocks, BOTH, split_axis=0, concat_axis=0, tiled=True)]
    all_to_all x1 -> x0, starting transfers between devices: 15.7 us -> none  [on_device(): lax.all_to_all(blocks, BOTH, split_axis=0, concat_axis=0, tiled=True)]
    reshape x6 -> x0, local copies, waits for them, and re-layouts: 7.09 us -> none  [the longest x1 3.14 us: on_device(): return blocks.transpose(2, 0, 3, 1, 4).reshape(stem.shape)]
  transfers between devices with their start and end apart: 2 -> 0, of which waited for: 1 -> 0; matrix products, arithmetic and copies ran while one was open for 1% -> 0% of each run, Pallas kernels for 0% -> 0%
where the time goes in v2:
time: 62.7 us; the launch traced here: 62.5 us
  Pallas kernels  59.1 us (94%)
  local copies, waits for them, and re-layouts  3.36 us (5%)
    pallas_call x1, Pallas kernels, on_device(): pl.pallas_call(kernel, out_shape=jax.ShapeDtypeStruct((1024, 128), F32),...  59.1 us
    unnamed x7, local copies, waits for them, and re-layouts  3.36 us

profile of v2, /device:TPU:1, one launch (start us, length us, event | category | flops | bytes accessed | tf_op | source)
XLA Modules:
  0.0 62.5 jit_solution(11118476640493164100)
XLA Ops:
  0.0 0.0 copy-start
  0.0 1.0 %copy-done = f32[2,1,1,256,1,256]{5,4,3,2,1,0:T(1,128)S(1)} copy-done((f32[2,1,1,256,1,256]{5,4,3,2,1,0:T(1,128)S(1)}, f32[2,1,1,256,1,256]{5,4,3,2,1,0:T(1,128)}, u32[]{:S(2)}) %copy-start) | copy-done | bytes 524312
  1.0 0.0 copy-start.1
  1.0 0.8 %copy-done.1 = f32[2,32,256]{2,1,0:T(8,128)S(1)} copy-done((f32[2,32,256]{2,1,0:T(8,128)S(1)}, f32[2,32,256]{2,1,0:T(8,128)}, u32[]{:S(2)}) %copy-start.1) | copy-done | bytes 65560
  1.9 0.0 copy-start.2
  1.9 0.7 %copy-done.2 = f32[2,2,1,256]{3,2,1,0:T(1,128)S(1)} copy-done((f32[2,2,1,256]{3,2,1,0:T(1,128)S(1)}, f32[2,2,1,256]{3,2,1,0:T(1,128)}, u32[]{:S(2)}) %copy-start.2) | copy-done | bytes 4120
  2.6 59.1 %absorb.1 = f32[1024,128]{1,0:T(8,128)S(1)} custom-call(f32[1024,128]{1,0:T(8,128)S(1)} %bitcast.4, f32[8,128]{1,0:T(8,128)S(1)} %bitcast.5, f32[2,32,256]{2,1,0:T(8,128)S(1)} %copy-done.1), custom_call_target="tpu_custom_call" | custom-call | tf_op jit(solution)/shard_map/absorb/pallas_call | solution.py:438
  61.7 0.8 %copy.6 = f32[2,1,1,256,1,256]{5,4,3,2,1,0:T(1,128)} copy(f32[2,1,1,256,1,256]{5,4,3,2,1,0:T(1,128)S(1)} %bitcast.3) | data formatting | bytes 1048576
Async XLA Ops:
  0.0 1.0 %copy-start = (f32[2,1,1,256,1,256]{5,4,3,2,1,0:T(1,128)S(1)}, f32[2,1,1,256,1,256]{5,4,3,2,1,0:T(1,128)}, u32[]{:S(2)}) copy-start(f32[2,1,1,256,1,256]{5,4,3,2,1,0:T(1,128)} %param.3) | copy-start | bytes 1572868
  1.0 0.8 %copy-start.1 = (f32[2,32,256]{2,1,0:T(8,128)S(1)}, f32[2,32,256]{2,1,0:T(8,128)}, u32[]{:S(2)}) copy-start(f32[2,32,256]{2,1,0:T(8,128)} %tail.1) | copy-start | bytes 196612
  1.9 0.7 %copy-start.2 = (f32[2,2,1,256]{3,2,1,0:T(1,128)S(1)}, f32[2,2,1,256]{3,2,1,0:T(1,128)}, u32[]{:S(2)}) copy-start(f32[2,2,1,256]{3,2,1,0:T(1,128)} %param.4) | copy-start | bytes 12292

commit v3 on v2

--- a/solution.py
+++ b/solution.py
@@ -10,10 +10,11 @@
 MESH = pl.DeviceIdType.MESH
 F32 = jnp.float32
 BF16 = jnp.bfloat16
+ORDER = ("z", "r0", "h", "t0", "r1", "r2", "t1", "t2", "t3", "t4", "r3", "g", "c")
 
 
 def rows(start, count=8):
-    return pl.ds(pl.multiple_of(start, 8), count)
+    return pl.ds(start if isinstance(start, int) else pl.multiple_of(start, 8), count)
 
 
 def device(z, y, x, core):
@@ -68,6 +69,7 @@
     xr,
     sent,
     got,
+    tails,
     ga,
     gb,
     wh,
@@ -80,6 +82,7 @@
     final,
     plane_sem,
     local_sem,
+    branch_sem,
     pair_send,
     pair_recv,
     z_send,
@@ -117,28 +120,41 @@
             local_sem.at[c],
         )
 
-    for c in range(2):
-        own_half(c).start()
-
     barrier = pltpu.get_barrier_semaphore()
-    pl.semaphore_signal(barrier, inc=1, device_id=sibling, device_id_type=MESH)
-    for d in range(1, 8):
-        pl.semaphore_signal(barrier, inc=1, device_id=device(at_z(d), y, x, core), device_id_type=MESH)
     for d in range(1, 16):
         pl.semaphore_signal(
             barrier, inc=1, device_id=device(z, at_y(d // 4), at_x(d % 4), core), device_id_type=MESH
         )
+    for d in range(1, 8):
+        pl.semaphore_signal(barrier, inc=1, device_id=device(at_z(d), y, x, core), device_id_type=MESH)
+    pl.semaphore_signal(barrier, inc=1, device_id=sibling, device_id_type=MESH)
 
     slot_a = ((core * 4 + y) * 8 + z) * 4 + x
-    slot_b = ((core * 4 + x) * 8 + z) * 4 + y
-    ga[rows(slot_a * 8), :] = pair[...]
-    line = lax.broadcasted_iota(jnp.int32, (8, 128), 0)
-    pieces = []
-    for c in range(2):
-        for h in range(2):
-            tile = tail[c, rows((z & 3) * 8), h * 128 : h * 128 + 128]
-            pieces.append(jnp.sum(jnp.where(line == core * 4 + x, tile, 0.0), axis=0, keepdims=True))
-    gb[rows(slot_b * 8), :] = jnp.concatenate([*pieces, jnp.zeros((4, 128), F32)], axis=0)
+    slot_b = (z * 4 + x) * 4 + y
+    fetches = [
+        pltpu.make_async_copy(tail, tails, branch_sem.at[0]),
+        pltpu.make_async_copy(pair, ga.at[rows(slot_a * 8)], branch_sem.at[1]),
+    ]
+    for fetch in fetches:
+        fetch.start()
+    for c in range(2):
+        own_half(c).start()
+
+    for fetch in fetches:
+        fetch.wait()
+    gathers_tail = (z >> 2) == core
+
+    @pl.when(gathers_tail)
+    def _():
+        line = lax.broadcasted_iota(jnp.int32, (8, 128), 0)
+        pieces = []
+        for f in range(2):
+            for c in range(2):
+                for h in range(2):
+                    tile = tails[c, rows(f * 16 + ((z >> 1) & 1) * 8), h * 128 : h * 128 + 128]
+                    tile = jnp.where(line == (z & 1) * 4 + x, tile, 0.0)
+                    pieces.append(jnp.sum(tile, axis=0, keepdims=True))
+        gb[rows(slot_b * 8), :] = jnp.concatenate(pieces, axis=0)
 
     pl.semaphore_wait(barrier, 23)
 
@@ -170,25 +186,14 @@
 
     for d in (4, 3, 5, 2, 6, 1, 7):
         along_z(ga, 0, slot_a, d).start()
-        along_z(gb, 1, slot_b, d).start()
-
-    for c in range(2):
-        own_half(c).wait()
-    for c in range(2):
-        half_across(c).wait()
-    pl.semaphore_wait(plane_sem, 7)
-
-    def block_ax(p):
-        return lambda lo, n: ga.reshape(2, 4, 8, 4, 8, 128).at[core, y, pl.ds(lo, n), p]
-
-    def block_by(p):
-        return lambda lo, n: gb.reshape(2, 4, 8, 4, 8, 128).at[core, x, pl.ds(lo, n), p]
-
-    def block_ay(p):
-        return lambda lo, n: ga.reshape(2, 4, 8, 4, 8, 128).at[core, p, pl.ds(lo, n)]
-
-    def block_bx(p):
-        return lambda lo, n: gb.reshape(2, 4, 8, 4, 8, 128).at[core, p, pl.ds(lo, n)]
+
+    @pl.when(gathers_tail)
+    def _():
+        for d in (4, 3, 5, 2, 6, 1, 7):
+            along_z(gb, 1, slot_b, d).start()
+
+    pairs = ga.reshape(2, 4, 2, 4, 4, 8, 128)
+    rests = gb.reshape(2, 2, 2, 4, 4, 8, 128)
 
     def on_x(d):
         return at_x(d), device(z, y, at_x(d), core)
@@ -196,51 +201,52 @@
     def on_y(d):
         return at_y(d), device(z, at_y(d), x, core)
 
-    def ring_copy(number, block, step, place, lo, n):
-        holder = place(0)[0] if step < 2 else place(-1 if step == 2 else 1)[0]
-        ref = block(holder)(lo, n)
+    def across(which, ref):
         return pltpu.make_async_remote_copy(
-            ref,
-            ref,
-            ring_send.at[number, step],
-            ring_recv.at[number, step],
-            device_id=place(1 if step in (0, 2) else -1)[1],
-            device_id_type=MESH,
-        )
-
-    def ring(number, block, place):
-        copies = [
-            ring_copy(number, block, 0, place, 0, 8),
-            ring_copy(number, block, 1, place, 0, 8),
-            ring_copy(number, block, 2, place, 0, 4),
-            ring_copy(number, block, 3, place, 4, 4),
-        ]
+            ref, ref, core_send.at[which], core_recv.at[which], device_id=sibling, device_id_type=MESH
+        )
+
+    def ring(number, block, place, which=None):
+        def copy(d, holder):
+            ref = block(place(holder)[0])
+            return pltpu.make_async_remote_copy(
+                ref,
+                ref,
+                ring_send.at[number, d - 1],
+                ring_recv.at[number, d - 1],
+                device_id=place(d)[1],
+                device_id_type=MESH,
+            )
+
+        def pass_on(holder):
+            if which is not None:
+                across(which, block(place(holder)[0])).start()
 
         def start():
-            copies[0].start()
-            copies[1].start()
-
-        def forward():
-            copies[0].wait_recv()
-            copies[2].start()
-            copies[1].wait_recv()
-            copies[3].start()
-
-        def finish():
-            copies[2].wait_recv()
-            copies[3].wait_recv()
+            for d in (2, 1, 3):
+                copy(d, 0).start()
+            pass_on(0)
+
+        def arrive():
+            for d in (1, 3, 2):
+                copy(d, -d).wait_recv()
+                pass_on(-d)
 
         def drain():
-            for copy in copies:
-                copy.wait_send()
-
-        return start, forward, finish, drain
+            for d in (1, 2, 3):
+                copy(d, 0).wait_send()
+
+        return start, arrive, drain
 
     rings = [
-        ring(0, block_ax, on_x),
-        ring(1, block_by, on_y),
-        ring(2, block_ay, on_y),
-        ring(3, block_bx, on_x),
+        ring(0, lambda p: pairs.at[core, y, 0, :, p], on_x),
+        ring(1, lambda p: pairs.at[core, p, 1, :, x], on_y),
+        ring(2, lambda p: rests.at[core, 0, :, p, y], on_x),
+        ring(3, lambda p: rests.at[core, 1, :, x, p], on_y),
+        ring(4, lambda p: pairs.at[core, p, 0], on_y, 0),
+        ring(5, lambda p: pairs.at[core, :, 1, :, p], on_x, 0),
+        ring(6, lambda p: rests.at[core, 0, :, :, p], on_y, 1),
+        ring(7, lambda p: rests.at[core, 1, :, p], on_x, 1),
     ]
 
     here = (((z & 3) * 4 + x) * 2 + (z >> 2)) * 4 + y
@@ -269,40 +275,77 @@
             for dy in range(4):
                 send_tile(number, zt, at_y(dy), xt)
 
-    send_groups(0, (4, 3, 5, 2, 6, 1, 7))
-    part = rows(0, 56)
-    for which, buffer in ((0, ga), (1, gb)):
-        pltpu.make_async_copy(buffer.at[part], buffer.at[part], z_recv.at[which]).wait()
-    rings[0][0]()
-    rings[1][0]()
-    send_groups(1, (4, 3, 5, 2, 6, 1, 7, 0))
-    rings[0][1]()
-    rings[1][1]()
-    send_groups(2, (4, 3, 5, 2, 6, 1, 7, 0))
-    rings[0][2]()
-    rings[1][2]()
-    rings[2][0]()
-    rings[3][0]()
-    send_groups(3, (4, 3, 5, 2, 6, 1, 7, 0))
-    shuffle_group(0, z, x)
-    for dy in range(1, 4):
-        send_tile(0, z, at_y(dy), x)
-    got[rows(here * 8), :] = sent[rows(y * 8), :]
-    rings[2][1]()
-    rings[3][1]()
-    rings[2][2]()
-    rings[3][2]()
-
-    def core_copy(which, buffer):
-        ref = buffer.at[rows(core * 1024, 1024)]
-        return pltpu.make_async_remote_copy(
-            ref, ref, core_send.at[which], core_recv.at[which], device_id=sibling, device_id_type=MESH
-        )
-
-    core_copy(0, ga).start()
-    core_copy(1, gb).start()
-    core_copy(0, ga).wait_recv()
-    core_copy(1, gb).wait_recv()
+    def wait_z():
+        part = rows(0, 56)
+        pltpu.make_async_copy(ga.at[part], ga.at[part], z_recv.at[0]).wait()
+
+        def wait_tail(count):
+            part = rows(0, count * 8)
+            pltpu.make_async_copy(gb.at[part], gb.at[part], z_recv.at[1]).wait()
+
+        @pl.when(gathers_tail)
+        def _():
+            wait_tail(3)
+
+        @pl.when(jnp.logical_not(gathers_tail))
+        def _():
+            wait_tail(4)
+
+    def wait_halves():
+        for c in range(2):
+            own_half(c).wait()
+        for c in range(2):
+            half_across(c).wait()
+        pl.semaphore_wait(plane_sem, 7)
+
+    def both(first, step):
+        for one in rings[first : first + 4]:
+            one[step]()
+
+    def tiles_near():
+        send_groups(0, (4, 3, 5, 2, 6, 1, 7))
+
+    def tiles_at(dx):
+        send_groups(dx, (4, 3, 5, 2, 6, 1, 7, 0))
+
+    def tiles_here():
+        shuffle_group(0, z, x)
+        for dy in range(1, 4):
+            send_tile(0, z, at_y(dy), x)
+        got[rows(here * 8), :] = sent[rows(y * 8), :]
+
+    def wait_across():
+        half_a, half_b = rows(other * 1024, 1024), rows(other * 512, 512)
+        pltpu.make_async_copy(ga.at[half_a], ga.at[half_a], core_recv.at[0]).wait()
+        pltpu.make_async_copy(gb.at[half_b], gb.at[half_b], core_recv.at[1]).wait()
+
+    def arrived():
+        part = rows(0, 127 * 8)
+        pltpu.make_async_copy(got.at[part], got.at[part], go_recv).wait()
+
+        for i in range(16):
+            for h in range(2):
+                tiles = [got[rows((i * 8 + h * 4 + j) * 8), :] for j in range(4)]
+                for k, tile in enumerate(swap_blocks(tiles)):
+                    x1[k % 2, rows(i * 16 + (k // 2) * 8), h * 128 : h * 128 + 128] = tile
+
+    steps = dict(
+        g=arrived,
+        z=wait_z,
+        h=wait_halves,
+        t0=tiles_near,
+        t1=functools.partial(tiles_at, 1),
+        t2=functools.partial(tiles_at, 2),
+        t3=functools.partial(tiles_at, 3),
+        t4=tiles_here,
+        r0=functools.partial(both, 0, 0),
+        r1=functools.partial(both, 0, 1),
+        r2=functools.partial(both, 4, 0),
+        r3=functools.partial(both, 4, 1),
+        c=wait_across,
+    )
+    for step in ORDER:
+        steps[step]()
 
     def weights(step, c):
         halves = []
@@ -314,11 +357,12 @@
     def tail_weights(c):
         halves = []
         for h in range(2):
-            k = c * 2 + h
             blocks = []
-            for i in range(32):
-                zi, yi = (i // 16) * 4 + i % 4, (i // 4) % 4
-                blocks.append(gb[pl.ds((zi * 4 + yi) * 8 + k, 8, stride=256), :])
+            for n in range(8):
+                for f in range(2):
+                    for j in range(2):
+                        start = ((n // 4) * 64 + j * 32 + n % 4) * 8 + f * 4 + c * 2 + h
+                        blocks.append(gb[pl.ds(start, 8, stride=32), :])
             halves.append(jnp.concatenate(blocks, axis=0))
         return jnp.concatenate(halves, axis=1)
 
@@ -326,16 +370,6 @@
         for step in range(2):
             wh[step, c], wl[step, c] = split(weights(step, c))
         wh[2, c], wl[2, c] = split(tail_weights(c).T)
-
-    part = rows(0, 127 * 8)
-    pltpu.make_async_copy(got.at[part], got.at[part], go_recv).wait()
-
-    @pl.loop(0, 16)
-    def _(i):
-        for h in range(2):
-            tiles = [got[rows((i * 8 + h * 4 + j) * 8), :] for j in range(4)]
-            for k, tile in enumerate(swap_blocks(tiles)):
-                x1[k % 2, rows(i * 16 + (k // 2) * 8), h * 128 : h * 128 + 128] = tile
 
     def weight(number, c):
         return wh[number, c], wl[number, c]
@@ -379,21 +413,17 @@
             device_id_type=MESH,
         ).start()
 
-    @pl.loop(0, 16)
-    def _(i):
+    for i in range(16):
         for dz in (4, 3, 5, 2, 6, 1, 7):
             send_back(at_z(dz), at_y(i & 3), at_x(i >> 2))
-
-        @pl.when(i > 0)
-        def _():
+        if i:
             send_back(z, at_y(i & 3), at_x(i >> 2))
 
     home[rows(there * 8), :] = back[rows(((y * 8 + z) * 4 + x) * 8), :]
     part = rows(0, 127 * 8)
     pltpu.make_async_copy(home.at[part], home.at[part], back_recv).wait()
 
-    @pl.loop(0, 16)
-    def _(i):
+    for i in range(16):
         for h in range(2):
             group = h * 16 + i
             tiles = [home[rows((group * 4 + j) * 8), :] for j in range(4)]
@@ -420,16 +450,37 @@
         out_across(c).start()
         out_here(c).start()
 
-    for which, buffer in ((0, ga), (1, gb)):
-        core_copy(which, buffer).wait_send()
-        pltpu.make_async_copy(buffer.at[rows(0, 56)], buffer.at[rows(0, 56)], z_send.at[which]).wait()
+    part = rows(0, 127 * 8)
+    half_a, half_b = rows(core * 1024, 1024), rows(core * 512, 512)
+    pltpu.make_async_copy(ga.at[half_a], ga.at[half_a], core_send.at[0]).wait()
+    pltpu.make_async_copy(gb.at[half_b], gb.at[half_b], core_send.at[1]).wait()
+    pltpu.make_async_copy(ga.at[rows(0, 56)], ga.at[rows(0, 56)], z_send.at[0]).wait()
+
+    @pl.when(gathers_tail)
+    def _():
+        pltpu.make_async_copy(gb.at[rows(0, 56)], gb.at[rows(0, 56)], z_send.at[1]).wait()
+
     for one in rings:
-        one[3]()
+        one[2]()
     pltpu.make_async_copy(sent.at[part], sent.at[part], go_send).wait()
     pltpu.make_async_copy(back.at[part], back.at[part], back_send).wait()
     for c in range(2):
         out_here(c).wait()
         out_across(c).wait()
+
+
+def hand_over(source, out, held, in_sem, out_sem):
+    size = source.shape[0] // in_sem.shape[0]
+    parts = [rows(i * size, size) for i in range(in_sem.shape[0])]
+    fetches = [pltpu.make_async_copy(source.at[p], held.at[p], in_sem.at[i]) for i, p in enumerate(parts)]
+    stores = [pltpu.make_async_copy(held.at[p], out.at[p], out_sem.at[i]) for i, p in enumerate(parts)]
+    for fetch in fetches:
+        fetch.start()
+    for fetch, store in zip(fetches, stores):
+        fetch.wait()
+        store.start()
+    for store in stores:
+        store.wait()
 
 
 def on_device(stem, branch_pair, branch_last):
@@ -439,17 +490,18 @@
         kernel,
         out_shape=jax.ShapeDtypeStruct((1024, 128), F32),
         in_specs=[
-            pl.BlockSpec(memory_space=pl.ANY),
-            pl.BlockSpec(memory_space=pltpu.VMEM),
-            pl.BlockSpec(memory_space=pltpu.VMEM),
+            pl.BlockSpec(memory_space=pltpu.HBM),
+            pl.BlockSpec(memory_space=pltpu.HBM),
+            pl.BlockSpec(memory_space=pltpu.HBM),
         ],
         out_specs=pl.BlockSpec(memory_space=pl.ANY),
         scratch_shapes=[
             whole,
             whole,
             whole,
+            pltpu.VMEM((2, 32, 256), F32),
             pltpu.VMEM((2048, 128), F32),
-            pltpu.VMEM((2048, 128), F32),
+            whole,
             pltpu.VMEM((3, 2, 256, 256), BF16),
             pltpu.VMEM((3, 2, 256, 256), BF16),
             pltpu.VMEM((2, 256, 256), F32),
@@ -464,8 +516,9 @@
             dma((2,)),
             dma((2,)),
             dma((2,)),
-            dma((4, 4)),
-            dma((4, 4)),
+            dma((2,)),
+            dma((8, 3)),
+            dma((8, 3)),
             dma((2,)),
             dma((2,)),
             dma,
@@ -475,9 +528,18 @@
             dma((2,)),
             dma((2,)),
         ],
-        compiler_params=pltpu.CompilerParams(collective_id=0, has_side_effects=True, vmem_limit_bytes=40 << 20),
+        compiler_params=pltpu.CompilerParams(collective_id=0, has_side_effects=True, vmem_limit_bytes=62 << 20),
         name="absorb",
     )(stem.reshape(1024, 128), branch_pair.reshape(8, 128), branch_last)
+    result = pl.pallas_call(
+        hand_over,
+        out_shape=jax.ShapeDtypeStruct((1024, 128), F32),
+        in_specs=[pl.BlockSpec(memory_space=pltpu.HBM)],
+        out_specs=pl.BlockSpec(memory_space=pltpu.HBM),
+        scratch_shapes=[whole, dma((4,)), dma((4,))],
+        compiler_params=pltpu.CompilerParams(vmem_limit_bytes=62 << 20),
+        name="hand_over",
+    )(result)
     return result.reshape(stem.shape)
 
 

time: 62.7 us -> 52.7 us (0.84)
  Pallas kernels: 59.1 us -> 52.6 us
  local copies, waits for them, and re-layouts: 3.36 us -> 0 us
    pallas_call x1, Pallas kernels: 59.1 us -> 50.8 us  [on_device(): pl.pallas_call(kernel, out_shape=jax.ShapeDtypeStruct((1024, 128), F32),...]
    unnamed x7 -> x0, local copies, waits for them, and re-layouts: 3.36 us -> none
    pallas_call x0 -> x1, Pallas kernels: none -> 1.82 us  [on_device(): pl.pallas_call(hand_over, out_shape=jax.ShapeDtypeStruct((1024, 128), F32...]
where the time goes in v3:
time: 52.7 us; the launch traced here: 52.6 us
  Pallas kernels  52.6 us (100%)
    pallas_call x1, Pallas kernels, on_device(): pl.pallas_call(kernel, out_shape=jax.ShapeDtypeStruct((1024, 128), F32),...  50.8 us
    pallas_call x1, Pallas kernels, on_device(): pl.pallas_call(hand_over, out_shape=jax.ShapeDtypeStruct((1024, 128), F32...  1.82 us

profile of v3, /device:TPU:1, one launch (start us, length us, event | category | flops | bytes accessed | tf_op | source)
XLA Modules:
  0.0 52.6 jit_solution(17346141149913899869)
XLA Ops:
  0.0 50.8 %absorb.1.source = f32[1024,128]{1,0:T(8,128)} custom-call(f32[1024,128]{1,0:T(8,128)} %bitcast.3, f32[8,128]{1,0:T(8,128)} %bitcast.4, f32[2,32,256]{2,1,0:T(8,128)} %tail.1), custom_call_target="tpu_custom_call" | custom-call | tf_op jit(solution)/shard_map/absorb/pallas_call | solution.py:489
  50.8 1.8 %hand_over.1 = f32[1024,128]{1,0:T(8,128)} custom-call(f32[1024,128]{1,0:T(8,128)} %absorb.1.source), custom_call_target="tpu_custom_call" | custom-call | tf_op jit(solution)/shard_map/hand_over/pallas_call | solution.py:534

commit v4 on v3

--- a/solution.py
+++ b/solution.py
@@ -10,7 +10,7 @@
 MESH = pl.DeviceIdType.MESH
 F32 = jnp.float32
 BF16 = jnp.bfloat16
-ORDER = ("z", "r0", "h", "t0", "r1", "r2", "t1", "t2", "t3", "t4", "r3", "g", "c")
+ORDER = ("h", "tp", "z", "r0", "p", "t0", "r1", "r2", "t1", "t2", "t3", "r3", "g", "c")
 
 
 def rows(start, count=8):
@@ -95,6 +95,7 @@
     go_recv,
     back_send,
     back_recv,
+    here_sem,
     out_send,
     out_recv,
 ):
@@ -121,12 +122,12 @@
         )
 
     barrier = pltpu.get_barrier_semaphore()
+    for d in (4, 3, 5, 2, 6, 1, 7):
+        pl.semaphore_signal(barrier, inc=1, device_id=device(at_z(d), y, x, core), device_id_type=MESH)
     for d in range(1, 16):
         pl.semaphore_signal(
             barrier, inc=1, device_id=device(z, at_y(d // 4), at_x(d % 4), core), device_id_type=MESH
         )
-    for d in range(1, 8):
-        pl.semaphore_signal(barrier, inc=1, device_id=device(at_z(d), y, x, core), device_id_type=MESH)
     pl.semaphore_signal(barrier, inc=1, device_id=sibling, device_id_type=MESH)
 
     slot_a = ((core * 4 + y) * 8 + z) * 4 + x
@@ -296,19 +297,21 @@
             own_half(c).wait()
         for c in range(2):
             half_across(c).wait()
+
+    def wait_planes():
         pl.semaphore_wait(plane_sem, 7)
 
     def both(first, step):
         for one in rings[first : first + 4]:
             one[step]()
 
-    def tiles_near():
-        send_groups(0, (4, 3, 5, 2, 6, 1, 7))
-
-    def tiles_at(dx):
-        send_groups(dx, (4, 3, 5, 2, 6, 1, 7, 0))
-
-    def tiles_here():
+    def tiles_to(dx):
+        send_groups(dx, (4, 3, 5, 2, 6, 1, 7))
+
+    def tiles_plane():
+        send_groups(1, (0,))
+        send_groups(2, (0,))
+        send_groups(3, (0,))
         shuffle_group(0, z, x)
         for dy in range(1, 4):
             send_tile(0, z, at_y(dy), x)
@@ -333,11 +336,12 @@
         g=arrived,
         z=wait_z,
         h=wait_halves,
-        t0=tiles_near,
-        t1=functools.partial(tiles_at, 1),
-        t2=functools.partial(tiles_at, 2),
-        t3=functools.partial(tiles_at, 3),
-        t4=tiles_here,
+        p=wait_planes,
+        tp=tiles_plane,
+        t0=functools.partial(tiles_to, 0),
+        t1=functools.partial(tiles_to, 1),
+        t2=functools.partial(tiles_to, 2),
+        t3=functools.partial(tiles_to, 3),
         r0=functools.partial(both, 0, 0),
         r1=functools.partial(both, 0, 1),
         r2=functools.partial(both, 4, 0),
@@ -403,52 +407,56 @@
 
     there = (z * 4 + x) * 4 + y
 
-    def send_back(zt, yt, xt):
+    def send_back(dz, yt, xt):
+        zt = at_z(dz)
         pltpu.make_async_remote_copy(
             back.at[rows(((yt * 8 + zt) * 4 + xt) * 8)],
             home.at[rows(there * 8)],
             back_send,
-            back_recv,
+            back_recv.at[dz & 3],
             device_id=device(zt, yt, xt, core),
             device_id_type=MESH,
         ).start()
 
-    for i in range(16):
-        for dz in (4, 3, 5, 2, 6, 1, 7):
-            send_back(at_z(dz), at_y(i & 3), at_x(i >> 2))
-        if i:
-            send_back(z, at_y(i & 3), at_x(i >> 2))
-
-    home[rows(there * 8), :] = back[rows(((y * 8 + z) * 4 + x) * 8), :]
-    part = rows(0, 127 * 8)
-    pltpu.make_async_copy(home.at[part], home.at[part], back_recv).wait()
-
-    for i in range(16):
-        for h in range(2):
-            group = h * 16 + i
-            tiles = [home[rows((group * 4 + j) * 8), :] for j in range(4)]
-            for j, tile in enumerate(swap_blocks(tiles)):
-                for gh in range(2):
-                    final[pl.ds(i * 16 + (gh * 4 + j) * 2 + h, 4, stride=256), :] = tile[gh * 4 : gh * 4 + 4]
-
-    def out_here(c):
+    for dzs in ((4, 2, 6, 0), (5, 3, 1, 7)):
+        for i in range(16):
+            for dz in dzs:
+                if i or dz:
+                    send_back(dz, at_y(i & 3), at_x(i >> 2))
+
+    def out_here(zl, j, c):
         return pltpu.make_async_copy(
-            final.at[rows(core * 512 + c * 256, 256)], out.at[rows(c * 512 + core * 256, 256)], local_sem.at[c]
-        )
-
-    def out_across(c):
+            final.at[rows(core * 512 + c * 256 + zl * 64, 64)],
+            out.at[rows(c * 512 + core * 256 + zl * 64, 64)],
+            here_sem.at[j, c],
+        )
+
+    def out_across(zl, j, c):
         return pltpu.make_async_remote_copy(
-            final.at[rows(other * 512 + c * 256, 256)],
-            out.at[rows(c * 512 + core * 256, 256)],
-            out_send.at[c],
-            out_recv.at[c],
+            final.at[rows(other * 512 + c * 256 + zl * 64, 64)],
+            out.at[rows(c * 512 + core * 256 + zl * 64, 64)],
+            out_send.at[j, c],
+            out_recv.at[j, c],
             device_id=sibling,
             device_id_type=MESH,
         )
 
-    for c in range(2):
-        out_across(c).start()
-        out_here(c).start()
+    home[rows(there * 8), :] = back[rows(((y * 8 + z) * 4 + x) * 8), :]
+    for j in (0, 2, 1, 3):
+        part = rows(0, (32 if j else 31) * 8)
+        pltpu.make_async_copy(home.at[part], home.at[part], back_recv.at[j]).wait()
+        zl = (z - j) & 3
+        for i in range(4):
+            for h in range(2):
+                group = (h * 4 + zl) * 4 + i
+                tiles = [home[rows((group * 4 + k) * 8), :] for k in range(4)]
+                for k, tile in enumerate(swap_blocks(tiles)):
+                    for gh in range(2):
+                        line = (zl * 4 + i) * 16 + (gh * 4 + k) * 2 + h
+                        final[pl.ds(line, 4, stride=256), :] = tile[gh * 4 : gh * 4 + 4]
+        for c in range(2):
+            out_across(zl, j, c).start()
+            out_here(zl, j, c).start()
 
     part = rows(0, 127 * 8)
     half_a, half_b = rows(core * 1024, 1024), rows(core * 512, 512)
@@ -464,9 +472,10 @@
         one[2]()
     pltpu.make_async_copy(sent.at[part], sent.at[part], go_send).wait()
     pltpu.make_async_copy(back.at[part], back.at[part], back_send).wait()
-    for c in range(2):
-        out_here(c).wait()
-        out_across(c).wait()
+    for j in range(4):
+        for c in range(2):
+            out_here((z - j) & 3, j, c).wait()
+            out_across((z - j) & 3, j, c).wait()
 
 
 def hand_over(source, out, held, in_sem, out_sem):
@@ -524,9 +533,10 @@
             dma,
             dma,
             dma,
-            dma,
-            dma((2,)),
-            dma((2,)),
+            dma((4,)),
+            dma((4, 2)),
+            dma((4, 2)),
+            dma((4, 2)),
         ],
         compiler_params=pltpu.CompilerParams(collective_id=0, has_side_effects=True, vmem_limit_bytes=62 << 20),
         name="absorb",

time: 52.7 us -> 51.9 us (0.985)
  Pallas kernels: 52.6 us -> 51.7 us
    pallas_call x1, Pallas kernels: 50.8 us -> 49.9 us  [on_device(): pl.pallas_call(kernel, out_shape=jax.ShapeDtypeStruct((1024, 128), F32),...]
where the time goes in v4:
time: 51.9 us; the launch traced here: 51.7 us
  Pallas kernels  51.7 us (100%)
    pallas_call x1, Pallas kernels, on_device(): pl.pallas_call(kernel, out_shape=jax.ShapeDtypeStruct((1024, 128), F32),...  49.9 us
    pallas_call x1, Pallas kernels, on_device(): pl.pallas_call(hand_over, out_shape=jax.ShapeDtypeStruct((1024, 128), F32...  1.82 us

profile of v4, /device:TPU:1, one launch (start us, length us, event | category | flops | bytes accessed | tf_op | source)
XLA Modules:
  0.0 51.7 jit_solution(2034833549699370665)
XLA Ops:
  0.0 49.9 %absorb.1.source = f32[1024,128]{1,0:T(8,128)} custom-call(f32[1024,128]{1,0:T(8,128)} %bitcast.3, f32[8,128]{1,0:T(8,128)} %bitcast.4, f32[2,32,256]{2,1,0:T(8,128)} %tail.1), custom_call_target="tpu_custom_call" | custom-call | tf_op jit(solution)/shard_map/absorb/pallas_call | solution.py:498
  49.9 1.8 %hand_over.1 = f32[1024,128]{1,0:T(8,128)} custom-call(f32[1024,128]{1,0:T(8,128)} %absorb.1.source), custom_call_target="tpu_custom_call" | custom-call | tf_op jit(solution)/shard_map/hand_over/pallas_call | solution.py:544

commit v5 on v4

--- a/solution.py
+++ b/solution.py
@@ -96,8 +96,7 @@
     back_send,
     back_recv,
     here_sem,
-    out_send,
-    out_recv,
+    own_sem,
 ):
     wide, narrow = lax.axis_index("wide"), lax.axis_index("narrow")
     core, x = wide & 1, (wide >> 1) & 3
@@ -401,49 +400,41 @@
         for k in range(2):
             for h in range(2):
                 for i in range(16):
-                    back[pl.ds(i * 64 + h * 4 + k * 2 + c, 8, stride=8), :] = third[c][
+                    back[pl.ds(i * 64 + k * 4 + h * 2 + c, 8, stride=8), :] = third[c][
                         k * 128 + i * 8 : k * 128 + i * 8 + 8, h * 128 : h * 128 + 128
                     ]
 
     there = (z * 4 + x) * 4 + y
 
-    def send_back(dz, yt, xt):
+    def half(tile, which):
+        return pl.ds(pl.multiple_of(tile * 8 + which * 4, 4), 4)
+
+    def send_back(dz, yt, xt, to_core):
         zt = at_z(dz)
         pltpu.make_async_remote_copy(
-            back.at[rows(((yt * 8 + zt) * 4 + xt) * 8)],
-            home.at[rows(there * 8)],
+            back.at[half((yt * 8 + zt) * 4 + xt, to_core)],
+            home.at[half(there, core)],
             back_send,
             back_recv.at[dz & 3],
-            device_id=device(zt, yt, xt, core),
+            device_id=device(zt, yt, xt, to_core),
             device_id_type=MESH,
         ).start()
 
     for dzs in ((4, 2, 6, 0), (5, 3, 1, 7)):
         for i in range(16):
             for dz in dzs:
-                if i or dz:
-                    send_back(dz, at_y(i & 3), at_x(i >> 2))
-
-    def out_here(zl, j, c):
-        return pltpu.make_async_copy(
-            final.at[rows(core * 512 + c * 256 + zl * 64, 64)],
-            out.at[rows(c * 512 + core * 256 + zl * 64, 64)],
-            here_sem.at[j, c],
-        )
-
-    def out_across(zl, j, c):
-        return pltpu.make_async_remote_copy(
-            final.at[rows(other * 512 + c * 256 + zl * 64, 64)],
-            out.at[rows(c * 512 + core * 256 + zl * 64, 64)],
-            out_send.at[j, c],
-            out_recv.at[j, c],
-            device_id=sibling,
-            device_id_type=MESH,
-        )
-
-    home[rows(there * 8), :] = back[rows(((y * 8 + z) * 4 + x) * 8), :]
+                for to_core in (core, other):
+                    if i or dz or to_core is other:
+                        send_back(dz, at_y(i & 3), at_x(i >> 2), to_core)
+    own = pltpu.make_async_copy(
+        back.at[half((y * 8 + z) * 4 + x, core)], home.at[half(there, core)], own_sem
+    )
+    own.start()
+    own.wait()
+
+    parts = out.reshape(2, 2, 4, 4, 2, 8, 128)
     for j in (0, 2, 1, 3):
-        part = rows(0, (32 if j else 31) * 8)
+        part = rows(0, 256) if j else pl.ds(0, 252)
         pltpu.make_async_copy(home.at[part], home.at[part], back_recv.at[j]).wait()
         zl = (z - j) & 3
         for i in range(4):
@@ -451,12 +442,13 @@
                 group = (h * 4 + zl) * 4 + i
                 tiles = [home[rows((group * 4 + k) * 8), :] for k in range(4)]
                 for k, tile in enumerate(swap_blocks(tiles)):
-                    for gh in range(2):
-                        line = (zl * 4 + i) * 16 + (gh * 4 + k) * 2 + h
-                        final[pl.ds(line, 4, stride=256), :] = tile[gh * 4 : gh * 4 + 4]
-        for c in range(2):
-            out_across(zl, j, c).start()
-            out_here(zl, j, c).start()
+                    final[pl.ds((zl * 4 + i) * 8 + k * 2 + h, 8, stride=128), :] = tile
+        for k in range(8):
+            pltpu.make_async_copy(
+                final.reshape(8, 4, 4, 8, 128).at[k, zl],
+                parts.at[k % 2, k // 4, zl, :, (k // 2) % 2],
+                here_sem,
+            ).start()
 
     part = rows(0, 127 * 8)
     half_a, half_b = rows(core * 1024, 1024), rows(core * 512, 512)
@@ -471,11 +463,9 @@
     for one in rings:
         one[2]()
     pltpu.make_async_copy(sent.at[part], sent.at[part], go_send).wait()
+    part = pl.ds(0, 1020)
     pltpu.make_async_copy(back.at[part], back.at[part], back_send).wait()
-    for j in range(4):
-        for c in range(2):
-            out_here((z - j) & 3, j, c).wait()
-            out_across((z - j) & 3, j, c).wait()
+    pltpu.make_async_copy(final, final, here_sem).wait()
 
 
 def hand_over(source, out, held, in_sem, out_sem):
@@ -534,9 +524,8 @@
             dma,
             dma,
             dma((4,)),
-            dma((4, 2)),
-            dma((4, 2)),
-            dma((4, 2)),
+            dma,
+            dma,
         ],
         compiler_params=pltpu.CompilerParams(collective_id=0, has_side_effects=True, vmem_limit_bytes=62 << 20),
         name="absorb",

time: 51.9 us -> 51.1 us (0.985)
  Pallas kernels: 51.7 us -> 51 us
    pallas_call x1, Pallas kernels: 49.9 us -> 49.2 us  [on_device(): pl.pallas_call(kernel, out_shape=jax.ShapeDtypeStruct((1024, 128), F32),...]
where the time goes in v5:
time: 51.1 us; the launch traced here: 51 us
  Pallas kernels  51 us (100%)
    pallas_call x1, Pallas kernels, on_device(): pl.pallas_call(kernel, out_shape=jax.ShapeDtypeStruct((1024, 128), F32),...  49.2 us
    pallas_call x1, Pallas kernels, on_device(): pl.pallas_call(hand_over, out_shape=jax.ShapeDtypeStruct((1024, 128), F32...  1.82 us

profile of v5, /device:TPU:1, one launch (start us, length us, event | category | flops | bytes accessed | tf_op | source)
XLA Modules:
  0.0 51.0 jit_solution(4648022098626413683)
XLA Ops:
  0.0 49.2 %absorb.1.source = f32[1024,128]{1,0:T(8,128)} custom-call(f32[1024,128]{1,0:T(8,128)} %bitcast.3, f32[8,128]{1,0:T(8,128)} %bitcast.4, f32[2,32,256]{2,1,0:T(8,128)} %tail.1), custom_call_target="tpu_custom_call" | custom-call | tf_op jit(solution)/shard_map/absorb/pallas_call | solution.py:488
  49.2 1.8 %hand_over.1 = f32[1024,128]{1,0:T(8,128)} custom-call(f32[1024,128]{1,0:T(8,128)} %absorb.1.source), custom_call_target="tpu_custom_call" | custom-call | tf_op jit(solution)/shard_map/hand_over/pallas_call | solution.py:533

commit v6 on v5

--- a/solution.py
+++ b/solution.py
@@ -79,7 +79,6 @@
     zz,
     back,
     home,
-    final,
     plane_sem,
     local_sem,
     branch_sem,
@@ -95,7 +94,6 @@
     go_recv,
     back_send,
     back_recv,
-    here_sem,
     own_sem,
 ):
     wide, narrow = lax.axis_index("wide"), lax.axis_index("narrow")
@@ -432,7 +430,6 @@
     own.start()
     own.wait()
 
-    parts = out.reshape(2, 2, 4, 4, 2, 8, 128)
     for j in (0, 2, 1, 3):
         part = rows(0, 256) if j else pl.ds(0, 252)
         pltpu.make_async_copy(home.at[part], home.at[part], back_recv.at[j]).wait()
@@ -442,13 +439,9 @@
                 group = (h * 4 + zl) * 4 + i
                 tiles = [home[rows((group * 4 + k) * 8), :] for k in range(4)]
                 for k, tile in enumerate(swap_blocks(tiles)):
-                    final[pl.ds((zl * 4 + i) * 8 + k * 2 + h, 8, stride=128), :] = tile
-        for k in range(8):
-            pltpu.make_async_copy(
-                final.reshape(8, 4, 4, 8, 128).at[k, zl],
-                parts.at[k % 2, k // 4, zl, :, (k // 2) % 2],
-                here_sem,
-            ).start()
+                    for q in range(4):
+                        line = (q // 2) * 256 + (zl * 4 + i) * 16 + ((q % 2) * 4 + k) * 2 + h
+                        out[pl.ds(line, 2, stride=512), :] = tile[q * 2 : q * 2 + 2]
 
     part = rows(0, 127 * 8)
     half_a, half_b = rows(core * 1024, 1024), rows(core * 512, 512)
@@ -465,35 +458,21 @@
     pltpu.make_async_copy(sent.at[part], sent.at[part], go_send).wait()
     part = pl.ds(0, 1020)
     pltpu.make_async_copy(back.at[part], back.at[part], back_send).wait()
-    pltpu.make_async_copy(final, final, here_sem).wait()
-
-
-def hand_over(source, out, held, in_sem, out_sem):
-    size = source.shape[0] // in_sem.shape[0]
-    parts = [rows(i * size, size) for i in range(in_sem.shape[0])]
-    fetches = [pltpu.make_async_copy(source.at[p], held.at[p], in_sem.at[i]) for i, p in enumerate(parts)]
-    stores = [pltpu.make_async_copy(held.at[p], out.at[p], out_sem.at[i]) for i, p in enumerate(parts)]
-    for fetch in fetches:
-        fetch.start()
-    for fetch, store in zip(fetches, stores):
-        fetch.wait()
-        store.start()
-    for store in stores:
-        store.wait()
 
 
 def on_device(stem, branch_pair, branch_last):
     dma = pltpu.SemaphoreType.DMA
+    in_hbm = functools.partial(pltpu.with_memory_space_constraint, memory_space=pltpu.HBM)
     whole = pltpu.VMEM((1024, 128), F32)
     result = pl.pallas_call(
         kernel,
-        out_shape=jax.ShapeDtypeStruct((1024, 128), F32),
+        out_shape=pltpu.VMEM((1024, 128), F32),
         in_specs=[
             pl.BlockSpec(memory_space=pltpu.HBM),
             pl.BlockSpec(memory_space=pltpu.HBM),
             pl.BlockSpec(memory_space=pltpu.HBM),
         ],
-        out_specs=pl.BlockSpec(memory_space=pl.ANY),
+        out_specs=pl.BlockSpec(memory_space=pltpu.VMEM),
         scratch_shapes=[
             whole,
             whole,
@@ -508,7 +487,6 @@
             pltpu.VMEM((4, 256, 128), F32),
             whole,
             whole,
-            whole,
             pltpu.SemaphoreType.REGULAR,
             dma((2,)),
             dma((2,)),
@@ -525,20 +503,10 @@
             dma,
             dma((4,)),
             dma,
-            dma,
         ],
-        compiler_params=pltpu.CompilerParams(collective_id=0, has_side_effects=True, vmem_limit_bytes=62 << 20),
+        compiler_params=pltpu.CompilerParams(collective_id=0, has_side_effects=True, vmem_limit_bytes=40 << 20),
         name="absorb",
-    )(stem.reshape(1024, 128), branch_pair.reshape(8, 128), branch_last)
-    result = pl.pallas_call(
-        hand_over,
-        out_shape=jax.ShapeDtypeStruct((1024, 128), F32),
-        in_specs=[pl.BlockSpec(memory_space=pltpu.HBM)],
-        out_specs=pl.BlockSpec(memory_space=pltpu.HBM),
-        scratch_shapes=[whole, dma((4,)), dma((4,))],
-        compiler_params=pltpu.CompilerParams(vmem_limit_bytes=62 << 20),
-        name="hand_over",
-    )(result)
+    )(in_hbm(stem.reshape(1024, 128)), in_hbm(branch_pair.reshape(8, 128)), in_hbm(branch_last))
     return result.reshape(stem.shape)
 
 

time: 51.1 us -> 49.5 us (0.969)
  Pallas kernels: 51 us -> 48.6 us
  local copies, waits for them, and re-layouts: 0 us -> 0.8 us
    pallas_call x2 -> x1, Pallas kernels: 51 us -> 48.6 us  [on_device(): pl.pallas_call(kernel, out_shape=pltpu.VMEM((1024, 128), F32), in_specs=[...]
    unnamed x0 -> x1, local copies, waits for them, and re-layouts: none -> 0.8 us
where the time goes in v6:
time: 49.5 us; the launch traced here: 49.4 us
  Pallas kernels  48.6 us (98%)
  local copies, waits for them, and re-layouts  0.8 us (2%)
    pallas_call x1, Pallas kernels, on_device(): pl.pallas_call(kernel, out_shape=pltpu.VMEM((1024, 128), F32), in_specs=[...  48.6 us

profile of v6, /device:TPU:1, one launch (start us, length us, event | category | flops | bytes accessed | tf_op | source)
XLA Modules:
  0.0 49.4 jit_solution(11989841994288644508)
XLA Ops:
  0.0 48.6 %absorb.1 = f32[1024,128]{1,0:T(8,128)S(1)} custom-call(f32[1024,128]{1,0:T(8,128)} %bitcast.4, f32[8,128]{1,0:T(8,128)} %bitcast.5, f32[2,32,256]{2,1,0:T(8,128)} %tail.1), custom_call_target="tpu_custom_call" | custom-call | tf_op jit(solution)/shard_map/absorb/pallas_call | solution.py:467
  48.6 0.8 %copy.6 = f32[2,1,1,256,1,256]{5,4,3,2,1,0:T(1,128)} copy(f32[2,1,1,256,1,256]{5,4,3,2,1,0:T(1,128)S(1)} %bitcast.3) | data formatting | bytes 1048576

commit v7 on v6

--- a/solution.py
+++ b/solution.py
@@ -10,7 +10,7 @@
 MESH = pl.DeviceIdType.MESH
 F32 = jnp.float32
 BF16 = jnp.bfloat16
-ORDER = ("h", "tp", "z", "r0", "p", "t0", "r1", "r2", "t1", "t2", "t3", "r3", "g", "c")
+ORDER = ("h", "tp", "z", "r0", "p", "t0", "r1", "t1", "t2", "t3", "r3", "g", "c", "w")
 
 
 def rows(start, count=8):
@@ -298,6 +298,11 @@
     def wait_planes():
         pl.semaphore_wait(plane_sem, 7)
 
+    def hand_on():
+        for i in range(4):
+            rings[i][1]()
+            rings[4 + i][0]()
+
     def both(first, step):
         for one in rings[first : first + 4]:
             one[step]()
@@ -316,8 +321,8 @@
 
     def wait_across():
         half_a, half_b = rows(other * 1024, 1024), rows(other * 512, 512)
+        pltpu.make_async_copy(gb.at[half_b], gb.at[half_b], core_recv.at[1]).wait()
         pltpu.make_async_copy(ga.at[half_a], ga.at[half_a], core_recv.at[0]).wait()
-        pltpu.make_async_copy(gb.at[half_b], gb.at[half_b], core_recv.at[1]).wait()
 
     def arrived():
         part = rows(0, 127 * 8)
@@ -328,25 +333,6 @@
                 tiles = [got[rows((i * 8 + h * 4 + j) * 8), :] for j in range(4)]
                 for k, tile in enumerate(swap_blocks(tiles)):
                     x1[k % 2, rows(i * 16 + (k // 2) * 8), h * 128 : h * 128 + 128] = tile
-
-    steps = dict(
-        g=arrived,
-        z=wait_z,
-        h=wait_halves,
-        p=wait_planes,
-        tp=tiles_plane,
-        t0=functools.partial(tiles_to, 0),
-        t1=functools.partial(tiles_to, 1),
-        t2=functools.partial(tiles_to, 2),
-        t3=functools.partial(tiles_to, 3),
-        r0=functools.partial(both, 0, 0),
-        r1=functools.partial(both, 0, 1),
-        r2=functools.partial(both, 4, 0),
-        r3=functools.partial(both, 4, 1),
-        c=wait_across,
-    )
-    for step in ORDER:
-        steps[step]()
 
     def weights(step, c):
         halves = []
@@ -367,10 +353,30 @@
             halves.append(jnp.concatenate(blocks, axis=0))
         return jnp.concatenate(halves, axis=1)
 
-    for c in range(2):
-        for step in range(2):
-            wh[step, c], wl[step, c] = split(weights(step, c))
-        wh[2, c], wl[2, c] = split(tail_weights(c).T)
+    def prepare():
+        for c in range(2):
+            for step in range(2):
+                wh[step, c], wl[step, c] = split(weights(step, c))
+            wh[2, c], wl[2, c] = split(tail_weights(c).T)
+
+    steps = dict(
+        g=arrived,
+        w=prepare,
+        z=wait_z,
+        h=wait_halves,
+        p=wait_planes,
+        tp=tiles_plane,
+        t0=functools.partial(tiles_to, 0),
+        t1=functools.partial(tiles_to, 1),
+        t2=functools.partial(tiles_to, 2),
+        t3=functools.partial(tiles_to, 3),
+        r0=functools.partial(both, 0, 0),
+        r1=hand_on,
+        r3=functools.partial(both, 4, 1),
+        c=wait_across,
+    )
+    for step in ORDER:
+        steps[step]()
 
     def weight(number, c):
         return wh[number, c], wl[number, c]

time: 49.5 us -> 49.1 us (level)
  no operation moved by 1% of the time
where the time goes in v7:
time: 49.1 us; the launch traced here: 49 us
  Pallas kernels  48.2 us (98%)
  local copies, waits for them, and re-layouts  0.8 us (2%)
    pallas_call x1, Pallas kernels, on_device(): pl.pallas_call(kernel, out_shape=pltpu.VMEM((1024, 128), F32), in_specs=[...  48.2 us

profile of v7, /device:TPU:1, one launch (start us, length us, event | category | flops | bytes accessed | tf_op | source)
XLA Modules:
  0.0 49.0 jit_solution(14895633114027142310)
XLA Ops:
  0.0 48.2 %absorb.1 = f32[1024,128]{1,0:T(8,128)S(1)} custom-call(f32[1024,128]{1,0:T(8,128)} %bitcast.4, f32[8,128]{1,0:T(8,128)} %bitcast.5, f32[2,32,256]{2,1,0:T(8,128)} %tail.1), custom_call_target="tpu_custom_call" | custom-call | tf_op jit(solution)/shard_map/absorb/pallas_call | solution.py:473
  48.2 0.8 %copy.6 = f32[2,1,1,256,1,256]{5,4,3,2,1,0:T(1,128)} copy(f32[2,1,1,256,1,256]{5,4,3,2,1,0:T(1,128)S(1)} %bitcast.3) | data formatting | bytes 1048576

commit v8 on v7

--- a/solution.py
+++ b/solution.py
@@ -79,6 +79,7 @@
     zz,
     back,
     home,
+    final,
     plane_sem,
     local_sem,
     branch_sem,
@@ -94,6 +95,7 @@
     go_recv,
     back_send,
     back_recv,
+    here_sem,
     own_sem,
 ):
     wide, narrow = lax.axis_index("wide"), lax.axis_index("narrow")
@@ -436,6 +438,7 @@
     own.start()
     own.wait()
 
+    parts = out.reshape(2, 2, 4, 4, 2, 8, 128)
     for j in (0, 2, 1, 3):
         part = rows(0, 256) if j else pl.ds(0, 252)
         pltpu.make_async_copy(home.at[part], home.at[part], back_recv.at[j]).wait()
@@ -445,9 +448,13 @@
                 group = (h * 4 + zl) * 4 + i
                 tiles = [home[rows((group * 4 + k) * 8), :] for k in range(4)]
                 for k, tile in enumerate(swap_blocks(tiles)):
-                    for q in range(4):
-                        line = (q // 2) * 256 + (zl * 4 + i) * 16 + ((q % 2) * 4 + k) * 2 + h
-                        out[pl.ds(line, 2, stride=512), :] = tile[q * 2 : q * 2 + 2]
+                    final[pl.ds((zl * 4 + i) * 8 + k * 2 + h, 8, stride=128), :] = tile
+        for k in range(8):
+            pltpu.make_async_copy(
+                final.reshape(8, 4, 4, 8, 128).at[k, zl],
+                parts.at[k % 2, k // 4, zl, :, (k // 2) % 2],
+                here_sem,
+            ).start()
 
     part = rows(0, 127 * 8)
     half_a, half_b = rows(core * 1024, 1024), rows(core * 512, 512)
@@ -464,6 +471,7 @@
     pltpu.make_async_copy(sent.at[part], sent.at[part], go_send).wait()
     part = pl.ds(0, 1020)
     pltpu.make_async_copy(back.at[part], back.at[part], back_send).wait()
+    pltpu.make_async_copy(final, final, here_sem).wait()
 
 
 def on_device(stem, branch_pair, branch_last):
@@ -493,6 +501,7 @@
             pltpu.VMEM((4, 256, 128), F32),
             whole,
             whole,
+            whole,
             pltpu.SemaphoreType.REGULAR,
             dma((2,)),
             dma((2,)),
@@ -508,6 +517,7 @@
             dma,
             dma,
             dma((4,)),
+            dma,
             dma,
         ],
         compiler_params=pltpu.CompilerParams(collective_id=0, has_side_effects=True, vmem_limit_bytes=40 << 20),

time: 49.1 us -> 49.2 us (level)
  no operation moved by 1% of the time
where the time goes in v8:
time: 49.2 us; the launch traced here: 49.1 us
  Pallas kernels  48.3 us (98%)
  local copies, waits for them, and re-layouts  0.8 us (2%)
    pallas_call x1, Pallas kernels, on_device(): pl.pallas_call(kernel, out_shape=pltpu.VMEM((1024, 128), F32), in_specs=[...  48.3 us

profile of v8, /device:TPU:1, one launch (start us, length us, event | category | flops | bytes accessed | tf_op | source)
XLA Modules:
  0.0 49.1 jit_solution(12522013623661405657)
XLA Ops:
  0.0 48.3 %absorb.1 = f32[1024,128]{1,0:T(8,128)S(1)} custom-call(f32[1024,128]{1,0:T(8,128)} %bitcast.4, f32[8,128]{1,0:T(8,128)} %bitcast.5, f32[2,32,256]{2,1,0:T(8,128)} %tail.1), custom_call_target="tpu_custom_call" | custom-call | tf_op jit(solution)/shard_map/absorb/pallas_call | solution.py:481
  48.3 0.8 %copy.6 = f32[2,1,1,256,1,256]{5,4,3,2,1,0:T(1,128)} copy(f32[2,1,1,256,1,256]{5,4,3,2,1,0:T(1,128)S(1)} %bitcast.3) | data formatting | bytes 1048576
